TPU v7x, 128 devices: a whole 4x4x4 slice. The times are simulated.
128 devices in a mesh: group: 2 (over core), member: 64 (over z, y, x).
Axes of the slice: x: 4, y: 4, z: 4, core: 2. Of those that a mesh axis runs over, the one named last changes fastest.
Arguments:
- embeddings: bfloat16 [65536, 1024], P(('group', 'member'))
- cluster: int32 [65536], P(('group', 'member')), may hold values from 0 to 7, as said below
Outputs:
- row_max: float32 [65536], P(('group', 'member'))
Inputs may be any that keep to these rules, and one draw needn't show every extreme that they name: Cluster c is owned by the 16 devices whose index over group and member together runs from c * 16 to c * 16 + 15. Among the rows of one device at most 96 lie in one cluster; in every draw one cluster holds exactly 96 rows of every device.
All inputs are finite; a program needn't handle non-finite values.
Results may differ from a plain program's by a relative error of at most 0.0005.
Values may be sent and summed in bfloat16 or wider, within the bound.
No kernel may reach another device: no remote copies, remote signals or barrier semaphores. Data moves between devices by JAX's collectives and lax.ppermute only.
A program may use at most 128 MiB of HBM per device.

v0:
```python
import functools

import jax
import jax.numpy as jnp
from jax import lax
from jax.experimental import pallas as pl
from jax.experimental.pallas import tpu as pltpu
from jax.sharding import PartitionSpec as P

AXES = ("group", "member")
SIDE = 4
CORES = 2
DEVICES = CORES * SIDE**3
BOUND = 96
HALF = SIDE * BOUND
SLOTS = CORES * HALF
TILE = 256
START = {"w": 0, "m": 0, "s": HALF}
STEPS = {
    "0": {"u": 0, "v": 0},
    "u1": {"u": 1},
    "u3": {"u": -1},
    "v1": {"v": 1},
    "u2": {"u": 2},
    "v2": {"v": 2},
}
BLOCKS = tuple(STEPS)
SECTIONS = 2 * SIDE
LANES = 128
CHUNKS = 4
EFFORT = 6
LOW = -8.0
NONE = -2.0


def place(device):
    return (device // 64, device // 16 % 4, device // 4 % 4, device % 4)


def device_at(core, z, y, x):
    return core * 64 + z % 4 * 16 + y % 4 * 4 + x % 4


def moved(device, core=0, ring=0, u=0, v=0):
    c, z, y, x = place(device)
    if c == 0:
        z, x, y = z + ring, x + u, y + v
    else:
        x, z, y = x + ring, z + u, y - v
    return device_at((c + core) % 2, z, y, x)


def take(block, **step):
    route = [(moved(device, **step), device) for device in range(DEVICES)]
    return lax.ppermute(block, AXES, route)


def here():
    member = lax.axis_index("member")
    return lax.axis_index("group"), member // 16, member // 4 % 4, member % 4


def partner(core, z, y, x, ring, u, v):
    ring = (jnp.where(core == 0, z, x) + ring) & 3
    u = (jnp.where(core == 0, x, z) + u) & 3
    y = (jnp.where(core == 0, y + v, y - v)) & 3
    return ring * jnp.where(core == 0, 16, 1) + u * jnp.where(core == 0, 1, 16) + y * 4


def sort_kernel(rows_hbm, cluster_hbm, mine_ref, other_ref, slot_ref, *scratch):
    rows_ref, cluster_ref, normed_ref, sems = scratch
    rows = rows_ref.shape[0]
    step = rows // CHUNKS
    copies = [pltpu.make_async_copy(cluster_hbm, cluster_ref, sems.at[CHUNKS])]
    for k in range(CHUNKS):
        part = pl.ds(k * step, step)
        copies.append(
            pltpu.make_async_copy(rows_hbm.at[part, :], rows_ref.at[part, :], sems.at[k])
        )
    for copy in copies:
        copy.start()
    core, z, y, x = here()
    ring_mine, ring_other = jnp.where(core == 0, z, x), jnp.where(core == 0, x, z)
    before = lax.broadcasted_iota(jnp.int32, (rows, rows), 0) < lax.broadcasted_iota(
        jnp.int32, (rows, rows), 1
    )
    before = jnp.where(before, 1.0, 0.0).astype(jnp.bfloat16)
    copies[0].wait()
    cluster = cluster_ref[...]
    hits = cluster == lax.broadcasted_iota(jnp.int32, (8, rows), 0)
    hits = jnp.where(hits, 1.0, 0.0)
    counted = jnp.dot(hits.astype(jnp.bfloat16), before, preferred_element_type=jnp.float32)
    rank = jnp.sum(counted * hits, 0, keepdims=True).astype(jnp.int32)
    is_mine = cluster // 4 == core
    turn = (cluster + 4 - jnp.where(is_mine, ring_mine, ring_other)) % 4
    slot = (jnp.where(is_mine, 0, 4) + turn) * BOUND + rank
    slot_ref[...] = slot
    for k in range(CHUNKS):
        copies[1 + k].wait()
        part = slice(k * step, (k + 1) * step)
        values = rows_ref[part, :].astype(jnp.float32)
        total = jnp.sum(values * values, 1, keepdims=True)
        normed_ref[part, :] = (values * lax.rsqrt(total + 1e-06)).astype(jnp.bfloat16)
    normed = normed_ref[...]
    for start, out_ref in ((0, mine_ref), (HALF, other_ref)):
        picks = slot - start == lax.broadcasted_iota(jnp.int32, (HALF, rows), 0)
        picks = jnp.where(picks, 1.0, 0.0)
        used = jnp.max(picks, 1, keepdims=True)
        placed = jnp.dot(picks.astype(jnp.bfloat16), normed, preferred_element_type=jnp.float32)
        first = lax.broadcasted_iota(jnp.int32, (HALF, LANES), 1) == 0
        head = jnp.where(first & (used < 0.5), 2.0, placed[:, :LANES])
        out_ref[:, :LANES] = head.astype(jnp.bfloat16)
        out_ref[:, LANES:] = placed[:, LANES:].astype(jnp.bfloat16)


def sort_rows(embeddings, cluster):
    rows, width = embeddings.shape
    vmem = pl.BlockSpec(memory_space=pltpu.VMEM)
    hbm = pl.BlockSpec(memory_space=pltpu.HBM)
    return pl.pallas_call(
        sort_kernel,
        in_specs=[hbm, hbm],
        out_specs=[vmem] * 3,
        out_shape=[
            jax.ShapeDtypeStruct((HALF, width), jnp.bfloat16),
            jax.ShapeDtypeStruct((HALF, width), jnp.bfloat16),
            jax.ShapeDtypeStruct((1, rows), jnp.int32),
        ],
        scratch_shapes=[
            pltpu.VMEM((rows, width), jnp.bfloat16),
            pltpu.VMEM((1, rows), jnp.int32),
            pltpu.VMEM((rows, width), jnp.bfloat16),
            pltpu.SemaphoreType.DMA((CHUNKS + 1,)),
        ],
        compiler_params=pltpu.CompilerParams(vmem_limit_bytes=20 << 20),
        cost_estimate=pl.CostEstimate(
            flops=4 * rows * HALF * width, bytes_accessed=6 * rows * width, transcendentals=rows
        ),
        name="sort_rows",
    )(embeddings, cluster)


def empty(values):
    return jnp.where(values[:, :LANES].astype(jnp.float32) > 1.5, LOW, 0.0)


def pair_kernel(names, blocks, products, *refs):
    chunks = dict(zip(names, refs))
    before_ref = refs[len(names)]
    best_ref, fold_ref, lane_ref = refs[-3:]
    fold_blocks = {upper for upper, parts, lower, kind, *tiles in products if kind != "lane"}
    lane_blocks = {lower for upper, parts, lower, kind, *tiles in products if kind != "fold"}
    for block in fold_blocks:
        fold_ref[blocks.index(block)] = jnp.full(fold_ref.shape[1:], LOW, jnp.float32)
    for block in lane_blocks:
        lane_ref[blocks.index(block)] = jnp.full(lane_ref.shape[1:], LOW, jnp.float32)
    for upper, parts, lower, kind, *tiles in products:
        for tile in tiles or range(SLOTS // TILE):
            columns = slice(tile * TILE, (tile + 1) * TILE)
            if tile == 0:
                right = chunks[lower, "m"][:TILE, :]
            elif tile == 1:
                first, second = chunks[lower, "m"], chunks[lower, "s"]
                right = jnp.concatenate([first[TILE:, :], second[: TILE // 2, :]], 0)
            else:
                right = chunks[lower, "s"][TILE // 2 :, :]
            if kind != "lane":
                across = empty(right).T[:1, :]
            for part in parts:
                values = chunks[upper, part][...]
                rows = values.shape[0]
                scores = lax.dot_general(
                    values, right, (((1,), (1,)), ((), ())), preferred_element_type=jnp.float32
                )
                if upper == lower:
                    row = lax.broadcasted_iota(jnp.int32, scores.shape, 0) + START[part]
                    column = lax.broadcasted_iota(jnp.int32, scores.shape, 1) + tile * TILE
                    scores = jnp.where(row == column, LOW, scores)
                if kind != "fold":
                    at = blocks.index(lower)
                    down = scores + empty(values)[:, :1]
                    down = jnp.max(down.reshape(rows // 8, 8, TILE), 0)
                    lane_ref[at, :, columns] = jnp.maximum(lane_ref[at, :, columns], down)
                if kind != "lane":
                    at = (blocks.index(upper), slice(START[part], START[part] + rows))
                    over = scores + across
                    over = jnp.maximum(over[:, :LANES], over[:, LANES:])
                    fold_ref[at] = jnp.maximum(fold_ref[at], over)
    best = [before_ref[k : k + 1, :] for k in range(len(BLOCKS))]
    for block in blocks:
        at, k = blocks.index(block), BLOCKS.index(block)
        if block in fold_blocks:
            best[k] = jnp.maximum(best[k], jnp.max(fold_ref[at].T, 0, keepdims=True))
        if block in lane_blocks:
            best[k] = jnp.maximum(best[k], jnp.max(lane_ref[at], 0, keepdims=True))
    if best_ref.shape[0] == len(BLOCKS):
        best_ref[...] = jnp.concatenate(best, 0)
        return
    best_ref[...] = jnp.full(best_ref.shape, NONE, jnp.float32)
    core, z, y, x = here()
    for section in range(SECTIONS):
        half, turn = section // SIDE, section % SIDE
        for k, step in enumerate(STEPS.values()):
            row = partner(core, z, y, x, -turn, step.get("u", 0), step.get("v", 0))
            row += (core if half == 0 else 1 - core) * 64
            best_ref[pl.ds(row, 1), :BOUND] = best[k][:, section * BOUND : (section + 1) * BOUND]


def pair_max(held, before, products, last, extra):
    names, blocks = [], []
    for upper, parts, lower, kind, *tiles in products:
        names += [(upper, part) for part in parts]
        names += [(lower, "m"), (lower, "s")]
        blocks += [lower] * (kind != "fold") + [upper] * (kind != "lane")
    names, blocks = list(dict.fromkeys(names)), list(dict.fromkeys(blocks))
    vmem = pl.BlockSpec(memory_space=pltpu.VMEM)
    width = held[names[0]].shape[1]
    pairs = sum(
        held[upper, part].shape[0] * (TILE * len(tiles) if tiles else SLOTS)
        for upper, parts, lower, kind, *tiles in products
        for part in parts
    )
    shape = (DEVICES, LANES) if last else before.shape
    return pl.pallas_call(
        functools.partial(pair_kernel, names, blocks, products),
        in_specs=[vmem] * (len(names) + 1)
        + [pl.BlockSpec(memory_space=pl.ANY)] * len(extra),
        out_specs=vmem,
        out_shape=jax.ShapeDtypeStruct(shape, jnp.float32),
        scratch_shapes=[
            pltpu.VMEM((len(blocks), SLOTS, LANES), jnp.float32),
            pltpu.VMEM((len(blocks), 8, SLOTS), jnp.float32),
        ],
        compiler_params=pltpu.CompilerParams(vmem_limit_bytes=20 << 20),
        cost_estimate=pl.CostEstimate(
            flops=2 * EFFORT * pairs * width,
            bytes_accessed=2 * len(names) * HALF * width,
            transcendentals=0,
        ),
        name="pair_max",
    )(*(held[name] for name in names), before, *extra)


def unsort_kernel(got_ref, slot_ref, out_ref, row_ref):
    rows = slot_ref.shape[1]
    core, z, y, x = here()
    row_ref[...] = jnp.full(row_ref.shape, NONE, jnp.float32)
    for section in range(SECTIONS):
        half, turn = section // SIDE, section % SIDE
        owner = core if half == 0 else 1 - core
        found = []
        for step in STEPS.values():
            row = partner(owner, z, y, x, turn, -step.get("u", 0), -step.get("v", 0))
            found.append(got_ref[pl.ds(row + owner * 64, 1), :])
        row_ref[section : section + 1, :] = functools.reduce(jnp.maximum, found)
    columns = row_ref[...].T
    best = jnp.full((1, rows), NONE, jnp.float32)
    for section in range(SECTIONS):
        place = lax.broadcasted_iota(jnp.int32, (BOUND, rows), 0) + section * BOUND
        found = jnp.where(slot_ref[...] == place, columns[:BOUND, section : section + 1], NONE)
        best = jnp.maximum(best, jnp.max(found, 0, keepdims=True))
    out_ref[...] = best


def unsort(got, slot):
    vmem = pl.BlockSpec(memory_space=pltpu.VMEM)
    return pl.pallas_call(
        unsort_kernel,
        in_specs=[vmem] * 2,
        out_specs=vmem,
        out_shape=jax.ShapeDtypeStruct(slot.shape, jnp.float32),
        scratch_shapes=[pltpu.VMEM((LANES, LANES), jnp.float32)],
        name="unsort",
    )(got, slot)


def on_device(embeddings, cluster):
    mine, other, slot = sort_rows(embeddings, cluster.reshape(1, -1))

    def section(block, step):
        return block[step * BOUND : (step + 1) * BOUND]

    held = {}
    near = {step: take(section(mine, step), ring=-step) for step in (2, 1, 3)}
    far = {step: take(section(other, step), core=1, ring=-step) for step in (2, 1, 3, 0)}
    near[0] = section(mine, 0)
    held["0", "m"] = jnp.concatenate([near[step] for step in range(SIDE)], 0)
    held["0", "s"] = jnp.concatenate([far[step] for step in range(SIDE)], 0)
    for part in "ms":
        held["v1", part] = take(held["0", part], v=1)
        held["u1", part] = take(held["0", part], u=1)
        held["u3", part] = take(held["0", part], u=-1)
    held["v2", "m"] = take(held["v1", "m"], v=1)
    held["v2", "s"] = take(held["v1", "s"], v=1)
    held["u2", "m"] = take(held["u3", "m"], u=-1)
    held["u2", "s"] = take(held["u1", "s"], u=1)

    plan = (
        ([("0", "ms", "0", "lane")], []),
        ([("v1", "m", "0", "both")], []),
        ([("u1", "m", "0", "both")], [held["u3", "m"]]),
        ([("v1", "s", "0", "both"), ("u1", "s", "0", "both")], []),
        ([("u1", "ms", "v1", "both"), ("u3", "ms", "v1", "both")], []),
        ([("v2", "m", "0", "both", 0, 1), ("v2", "m", "u1", "both")], []),
        ([("u2", "m", "0", "lane", 0, 1), ("u2", "m", "v1", "both")], []),
        (
            [
                ("u2", "s", "0", "both"),
                ("u2", "s", "v1", "both"),
                ("v2", "m", "u2", "both", 0, 1),
            ],
            [],
        ),
        ([("v2", "s", near, "both") for near in ("0", "u1", "u2")], []),
    )
    best = jnp.full((len(BLOCKS), SLOTS), NONE, jnp.float32)
    for k, (products, extra) in enumerate(plan):
        best = pair_max(held, best, products, k + 1 == len(plan), extra)
    got = lax.all_to_all(best, AXES, 0, 0, tiled=True)
    return unsort(got, slot).reshape(-1)


def solution(mesh):
    in_specs = (P(AXES, None), P(AXES))
    return jax.shard_map(
        on_device, mesh=mesh, in_specs=in_specs, out_specs=P(AXES), check_vma=False
    )
```

profile of v0, /device:TPU:1, one launch (start us, length us, event | category | flops | bytes accessed | tf_op | source)
XLA Modules:
  0.0 77.8 jit_solution(6028247731361014378)
XLA Ops:
  0.0 1.2 %copy-done.1 = bf16[512,1024]{1,0:T(8,128)(2,1)S(1)} copy-done((bf16[512,1024]{1,0:T(8,128)(2,1)S(1)}, bf16[512,1024]{1,0:T(8,128)(2,1)}, u32[]{:S(2)}) %copy-start.1) | copy-done | bytes 1048600
  1.2 0.7 copy-done.2
  1.9 1.9 %sort_rows.1 = (bf16[384,1024]{1,0:T(8,128)(2,1)S(1)}, bf16[384,1024]{1,0:T(8,128)(2,1)S(1)}, s32[1,512]{1,0:T(1,128)S(1)}) custom-call(bf16[512,1024]{1,0:T(8,128)(2,1)S(1)} %copy-done.1, s32[1,512]{1,0:T(1,128)S(1)} %bitcast.7), custom_call_target="tpu_custom_call" | custom-call | flops 805306368 | bytes 3145728 | tf_op jit(solution)/shard_map/sort_rows/pallas_call | solution.py:120
  3.8 0.1 fusion
  3.9 2.1 %collective-permute-start.6 = (bf16[96,1024]{1,0:T(8,128)(2,1)S(1)}, bf16[96,1024]{1,0:T(8,128)(2,1)S(1)}, u32[]{:S(2)}, u32[]{:S(2)}) collective-permute-start(bf16[96,1024]{1,0:T(8,128)(2,1)S(1)} %get-tuple-element.14), channel_id=1, source_target_pairs={{48,0},{49,1},{50,2},{51,3},{52,4},{53,5},{54,6},{55,7},{56,8},{57... | collective-permute-start | bytes 589832 | tf_op jit(solution)/shard_map/ppermute | solution.py:55
  6.0 2.5 %collective-permute-start.7 = (bf16[96,1024]{1,0:T(8,128)(2,1)S(1)}, bf16[96,1024]{1,0:T(8,128)(2,1)S(1)}, u32[]{:S(2)}, u32[]{:S(2)}) collective-permute-start(bf16[96,1024]{1,0:T(8,128)(2,1)S(1)} %get-tuple-element.13), channel_id=1, source_target_pairs={{32,0},{33,1},{34,2},{35,3},{36,4},{37,5},{38,6},{39,7},{40,8},{41... | collective-permute-start | bytes 589832 | tf_op jit(solution)/shard_map/ppermute | solution.py:55
  8.4 1.2 %collective-permute-start.8 = (bf16[96,1024]{1,0:T(8,128)(2,1)S(1)}, bf16[96,1024]{1,0:T(8,128)(2,1)S(1)}, u32[]{:S(2)}, u32[]{:S(2)}) collective-permute-start(bf16[96,1024]{1,0:T(8,128)(2,1)S(1)} %get-tuple-element.12), channel_id=1, source_target_pairs={{16,0},{17,1},{18,2},{19,3},{20,4},{21,5},{22,6},{23,7},{24,8},{25... | collective-permute-start | bytes 589832 | tf_op jit(solution)/shard_map/ppermute | solution.py:55
  9.6 0.1 fusion.1
  9.7 2.5 %collective-permute-start = (bf16[96,1024]{1,0:T(8,128)(2,1)S(1)}, bf16[96,1024]{1,0:T(8,128)(2,1)S(1)}, u32[]{:S(2)}, u32[]{:S(2)}) collective-permute-start(bf16[96,1024]{1,0:T(8,128)(2,1)S(1)} %get-tuple-element.18), channel_id=1, source_target_pairs={{64,0},{65,1},{66,2},{67,3},{68,4},{69,5},{70,6},{71,7},{72,8},{73... | collective-permute-start | bytes 589832 | tf_op jit(solution)/shard_map/ppermute | solution.py:55
  12.1 0.7 collective-permute-start.1
  12.8 0.0 collective-permute-done.6
  12.8 1.8 %collective-permute-start.2 = (bf16[96,1024]{1,0:T(8,128)(2,1)S(1)}, bf16[96,1024]{1,0:T(8,128)(2,1)S(1)}, u32[]{:S(2)}, u32[]{:S(2)}) collective-permute-start(bf16[96,1024]{1,0:T(8,128)(2,1)S(1)} %get-tuple-element.16), channel_id=1, source_target_pairs={{96,0},{97,1},{98,2},{99,3},{100,4},{101,5},{102,6},{103,7},{104,8... | collective-permute-start | bytes 589832 | tf_op jit(solution)/shard_map/ppermute | solution.py:55
  14.6 0.0 collective-permute-done.7
  14.6 3.2 %collective-permute-start.3 = (bf16[96,1024]{1,0:T(8,128)(2,1)S(1)}, bf16[96,1024]{1,0:T(8,128)(2,1)S(1)}, u32[]{:S(2)}, u32[]{:S(2)}) collective-permute-start(bf16[96,1024]{1,0:T(8,128)(2,1)S(1)} %get-tuple-element.15), channel_id=1, source_target_pairs={{80,0},{81,1},{82,2},{83,3},{84,4},{85,5},{86,6},{87,7},{88,8},{89... | collective-permute-start | bytes 589832 | tf_op jit(solution)/shard_map/ppermute | solution.py:55
  17.8 0.0 collective-permute-done.8
  17.8 0.1 pad_maximum_fusion.refs_0_.refs_1_
  17.8 1.4 %collective-permute-start.14 = (bf16[384,1024]{1,0:T(8,128)(2,1)S(1)}, bf16[384,1024]{1,0:T(8,128)(2,1)S(1)}, u32[]{:S(2)}, u32[]{:S(2)}) collective-permute-start(bf16[384,1024]{1,0:T(8,128)(2,1)S(1)} %pad_maximum_fusion.refs_0_.refs_1_), channel_id=1, source_target_pairs={{4,0},{5,1},{6,2},{7,3},{8,4},{9,5},{10,6},{11,7},{12,8},{13,9},{1... | collective-permute-start | bytes 2359304 | tf_op jit(solution)/shard_map/ppermute | solution.py:55
  19.2 0.0 collective-permute-done
  19.2 0.6 collective-permute-start.9
  19.8 0.0 collective-permute-done.1
  19.8 0.9 %collective-permute-start.11 = (bf16[384,1024]{1,0:T(8,128)(2,1)S(1)}, bf16[384,1024]{1,0:T(8,128)(2,1)S(1)}, u32[]{:S(2)}, u32[]{:S(2)}) collective-permute-start(bf16[384,1024]{1,0:T(8,128)(2,1)S(1)} %pad_maximum_fusion.refs_0_.refs_1_), channel_id=1, source_target_pairs={{3,0},{0,1},{1,2},{2,3},{7,4},{4,5},{5,6},{6,7},{11,8},{8,9},{9,10... | collective-permute-start | bytes 2359304 | tf_op jit(solution)/shard_map/ppermute | solution.py:55
  20.8 0.7 collective-permute-done.2
  21.5 0.7 collective-permute-done.3
  22.3 1.6 %collective-permute-start.10 = (bf16[384,1024]{1,0:T(8,128)(2,1)S(1)}, bf16[384,1024]{1,0:T(8,128)(2,1)S(1)}, u32[]{:S(2)}, u32[]{:S(2)}) collective-permute-start(bf16[384,1024]{1,0:T(8,128)(2,1)S(1)} %constant_dynamic-update-slice_fusion.refs_1_.refs_2_), channel_id=1, source_target_pairs={{1,0},{2,1},{3,2},{0,3},{5,4},{6,5},{7,6},{4,7},{9,8},{10,9},{11,1... | collective-permute-start | bytes 2359304 | tf_op jit(solution)/shard_map/ppermute | solution.py:55
  23.9 1.3 %collective-permute-start.4 = (bf16[384,1024]{1,0:T(8,128)(2,1)S(1)}, bf16[384,1024]{1,0:T(8,128)(2,1)S(1)}, u32[]{:S(2)}, u32[]{:S(2)}) collective-permute-start(bf16[384,1024]{1,0:T(8,128)(2,1)S(1)} %constant_dynamic-update-slice_fusion.refs_1_.refs_2_), channel_id=1, source_target_pairs={{4,0},{5,1},{6,2},{7,3},{8,4},{9,5},{10,6},{11,7},{12,8},{13,9},{1... | collective-permute-start | bytes 2359304 | tf_op jit(solution)/shard_map/ppermute | solution.py:55
  25.2 1.5 %pair_max.9.refs_3_ = f32[6,768]{1,0:T(8,128)S(1)} custom-call(bf16[384,1024]{1,0:T(8,128)(2,1)S(1)} %pad_maximum_fusion.refs_0_.refs_1_, bf16[384,1024]{1,0:T(8,128)(2,1)S(1)} %constant_dynamic-update-slice_fusion.refs_1_.refs_2_, f32[6,768]{1,0:T(8,128)S(1)} %broadcast_in_dim.3.refs_2_), custom_call_target="tpu_custom_call" | custom-call | flops 7247757312 | bytes 1572864 | tf_op jit(solution)/shard_map/pair_max/pallas_call | solution.py:224
  26.7 3.6 %collective-permute-done.14.refs_0_.refs_2_.refs_3_ = bf16[384,1024]{1,0:T(8,128)(2,1)S(1)} collective-permute-done((bf16[384,1024]{1,0:T(8,128)(2,1)S(1)}, bf16[384,1024]{1,0:T(8,128)(2,1)S(1)}, u32[]{:S(2)}, u32[]{:S(2)}) %collective-permute-start.14) | collective-permute-done | bytes 786464 | tf_op jit(solution)/shard_map/ppermute | solution.py:55
  30.3 0.3 collective-permute-start.16
  30.6 1.0 %pair_max.10.refs_3_ = f32[6,768]{1,0:T(8,128)S(1)} custom-call(bf16[384,1024]{1,0:T(8,128)(2,1)S(1)} %collective-permute-done.14.refs_0_.refs_2_.refs_3_, bf16[384,1024]{1,0:T(8,128)(2,1)S(1)} %pad_maximum_fusion.refs_0_.refs_1_, bf16[384,1024]{1,0:T(8,128)(2,1)S(1)} %constant_dynamic-update-slice_fusion.refs_1_.refs_2_, f32[6,768]{1,0:T(8,128)S(1)} %pair_max.9.refs_3_), custom_call_target="tpu_custom_call" | custom-call | flops 3623878656 | bytes 2359296 | tf_op jit(solution)/shard_map/pair_max/pallas_call | solution.py:224
  31.6 0.0 collective-permute-done.9.refs_0_.refs_3_
  31.6 0.1 collective-permute-start.15
  31.7 0.5 collective-permute-done.11.refs_4_
  32.2 0.2 collective-permute-start.12
  32.5 6.3 %collective-permute-done.10.refs_3_.refs_1_.refs_4_ = bf16[384,1024]{1,0:T(8,128)(2,1)S(1)} collective-permute-done((bf16[384,1024]{1,0:T(8,128)(2,1)S(1)}, bf16[384,1024]{1,0:T(8,128)(2,1)S(1)}, u32[]{:S(2)}, u32[]{:S(2)}) %collective-permute-start.10) | collective-permute-done | bytes 786464 | tf_op jit(solution)/shard_map/ppermute | solution.py:55
  38.8 1.9 %collective-permute-start.13 = (bf16[384,1024]{1,0:T(8,128)(2,1)S(1)}, bf16[384,1024]{1,0:T(8,128)(2,1)S(1)}, u32[]{:S(2)}, u32[]{:S(2)}) collective-permute-start(bf16[384,1024]{1,0:T(8,128)(2,1)S(1)} %collective-permute-done.10.refs_3_.refs_1_.refs_4_), channel_id=1, source_target_pairs={{1,0},{2,1},{3,2},{0,3},{5,4},{6,5},{7,6},{4,7},{9,8},{10,9},{11,1... | collective-permute-start | bytes 2359304 | tf_op jit(solution)/shard_map/ppermute | solution.py:55
  40.7 1.3 %collective-permute-start.5 = (bf16[384,1024]{1,0:T(8,128)(2,1)S(1)}, bf16[384,1024]{1,0:T(8,128)(2,1)S(1)}, u32[]{:S(2)}, u32[]{:S(2)}) collective-permute-start(bf16[384,1024]{1,0:T(8,128)(2,1)S(1)} %collective-permute-done.4.refs_0_.refs_3_.refs_4_), channel_id=1, source_target_pairs={{4,0},{5,1},{6,2},{7,3},{8,4},{9,5},{10,6},{11,7},{12,8},{13,9},{1... | collective-permute-start | bytes 2359304 | tf_op jit(solution)/shard_map/ppermute | solution.py:55
  42.0 1.0 %pair_max.11.refs_4_ = f32[6,768]{1,0:T(8,128)S(1)} custom-call(bf16[384,1024]{1,0:T(8,128)(2,1)S(1)} %collective-permute-done.9.refs_0_.refs_3_, bf16[384,1024]{1,0:T(8,128)(2,1)S(1)} %pad_maximum_fusion.refs_0_.refs_1_, bf16[384,1024]{1,0:T(8,128)(2,1)S(1)} %constant_dynamic-update-slice_fusion.refs_1_.refs_2_, f32[6,768]{1,0:T(8,128)S(1)} %pair_max.10.refs_3_, ...), custom_call_target="tpu_custom_call" | custom-call | flops 3623878656 | bytes 2359296 | tf_op jit(solution)/shard_map/pair_max/pallas_call | solution.py:224
  42.9 1.6 %pair_max.12.refs_6_ = f32[6,768]{1,0:T(8,128)S(1)} custom-call(bf16[384,1024]{1,0:T(8,128)(2,1)S(1)} %collective-permute-done.4.refs_0_.refs_3_.refs_4_, bf16[384,1024]{1,0:T(8,128)(2,1)S(1)} %pad_maximum_fusion.refs_0_.refs_1_, bf16[384,1024]{1,0:T(8,128)(2,1)S(1)} %constant_dynamic-update-slice_fusion.refs_1_.refs_2_, ...), custom_call_target="tpu_custom_call" | custom-call | flops 7247757312 | bytes 3145728 | tf_op jit(solution)/shard_map/pair_max/pallas_call | solution.py:224
  44.6 3.1 %pair_max.13.refs_5_ = f32[6,768]{1,0:T(8,128)S(1)} custom-call(bf16[384,1024]{1,0:T(8,128)(2,1)S(1)} %collective-permute-done.9.refs_0_.refs_3_, bf16[384,1024]{1,0:T(8,128)(2,1)S(1)} %collective-permute-done.10.refs_3_.refs_1_.refs_4_, bf16[384,1024]{1,0:T(8,128)(2,1)S(1)} %collective-permute-done.14.refs_0_.refs_2_.refs_3_, ...), custom_call_target="tpu_custom_call" | custom-call | flops 14495514624 | bytes 4718592 | tf_op jit(solution)/shard_map/pair_max/pallas_call | solution.py:224
  47.7 0.0 collective-permute-done.15.refs_0_.refs_5_
  47.7 1.5 %pair_max.14.refs_5_ = f32[6,768]{1,0:T(8,128)S(1)} custom-call(bf16[384,1024]{1,0:T(8,128)(2,1)S(1)} %collective-permute-done.15.refs_0_.refs_5_, bf16[384,1024]{1,0:T(8,128)(2,1)S(1)} %pad_maximum_fusion.refs_0_.refs_1_, bf16[384,1024]{1,0:T(8,128)(2,1)S(1)} %constant_dynamic-update-slice_fusion.refs_1_.refs_2_, ...), custom_call_target="tpu_custom_call" | custom-call | flops 6039797760 | bytes 3932160 | tf_op jit(solution)/shard_map/pair_max/pallas_call | solution.py:224
  49.1 2.0 %collective-permute-done.12.refs_0_.refs_6_.refs_5_ = bf16[384,1024]{1,0:T(8,128)(2,1)S(1)} collective-permute-done((bf16[384,1024]{1,0:T(8,128)(2,1)S(1)}, bf16[384,1024]{1,0:T(8,128)(2,1)S(1)}, u32[]{:S(2)}, u32[]{:S(2)}) %collective-permute-start.12) | collective-permute-done | bytes 786464 | tf_op jit(solution)/shard_map/ppermute | solution.py:55
  51.1 1.4 %pair_max.15.refs_7_ = f32[6,768]{1,0:T(8,128)S(1)} custom-call(bf16[384,1024]{1,0:T(8,128)(2,1)S(1)} %collective-permute-done.12.refs_0_.refs_6_.refs_5_, bf16[384,1024]{1,0:T(8,128)(2,1)S(1)} %pad_maximum_fusion.refs_0_.refs_1_, bf16[384,1024]{1,0:T(8,128)(2,1)S(1)} %constant_dynamic-update-slice_fusion.refs_1_.refs_2_, ...), custom_call_target="tpu_custom_call" | custom-call | flops 6039797760 | bytes 3932160 | tf_op jit(solution)/shard_map/pair_max/pallas_call | solution.py:224
  52.5 2.1 %pair_max.16.refs_7_ = f32[6,768]{1,0:T(8,128)S(1)} custom-call(bf16[384,1024]{1,0:T(8,128)(2,1)S(1)} %collective-permute-done.13.refs_0_.refs_6_, bf16[384,1024]{1,0:T(8,128)(2,1)S(1)} %pad_maximum_fusion.refs_0_.refs_1_, bf16[384,1024]{1,0:T(8,128)(2,1)S(1)} %constant_dynamic-update-slice_fusion.refs_1_.refs_2_, ...), custom_call_target="tpu_custom_call" | custom-call | flops 9663676416 | bytes 5505024 | tf_op jit(solution)/shard_map/pair_max/pallas_call | solution.py:224
  54.6 0.7 collective-permute-done.5.refs_0_
  55.3 2.5 %pair_max.17 = f32[128,128]{1,0:T(8,128)S(1)} custom-call(bf16[384,1024]{1,0:T(8,128)(2,1)S(1)} %collective-permute-done.5.refs_0_, bf16[384,1024]{1,0:T(8,128)(2,1)S(1)} %pad_maximum_fusion.refs_0_.refs_1_, bf16[384,1024]{1,0:T(8,128)(2,1)S(1)} %constant_dynamic-update-slice_fusion.refs_1_.refs_2_, ...), custom_call_target="tpu_custom_call" | custom-call | flops 10871635968 | bytes 5505024 | tf_op jit(solution)/shard_map/pair_max/pallas_call | solution.py:224
  57.8 18.1 %all_to_all.11 = f32[128,1,128]{2,1,0:T(1,128)} all-to-all(f32[128,1,128]{2,1,0:T(1,128)S(1)} %bitcast.6), channel_id=1, replica_groups=mesh['group'=2,'member'=64] {'group','member'}, dimensions={0} | all-to-all | bytes 131072 | tf_op jit(solution)/shard_map/all_to_all | solution.py:319
  75.9 1.8 %unsort.1 = f32[1,512]{1,0:T(1,128)} custom-call(f32[128,128]{1,0:T(8,128)} %bitcast.8, s32[1,512]{1,0:T(1,128)} %copy-done), custom_call_target="tpu_custom_call" | custom-call | tf_op jit(solution)/shard_map/unsort/pallas_call | solution.py:267
  (12 shorter events, 0.1 us)
Async XLA Ops:
  0.0 1.2 %copy-start.1 = (bf16[512,1024]{1,0:T(8,128)(2,1)S(1)}, bf16[512,1024]{1,0:T(8,128)(2,1)}, u32[]{:S(2)}) copy-start(bf16[512,1024]{1,0:T(8,128)(2,1)} %rows_hbm.1) | copy-start | bytes 3145732
  1.2 0.7 copy-start.2
  3.8 5.8 %copy-start = (s32[1,512]{1,0:T(1,128)}, s32[1,512]{1,0:T(1,128)S(1)}, u32[]{:S(2)}) copy-start(s32[1,512]{1,0:T(1,128)S(1)} %get-tuple-element.10.slot_ref) | copy-start | bytes 6148
  3.9 8.9 %collective-permute-start.6 = (bf16[96,1024]{1,0:T(8,128)(2,1)S(1)}, bf16[96,1024]{1,0:T(8,128)(2,1)S(1)}, u32[]{:S(2)}, u32[]{:S(2)}) collective-permute-start(bf16[96,1024]{1,0:T(8,128)(2,1)S(1)} %get-tuple-element.14), channel_id=1, source_target_pairs={{48,0},{49,1},{50,2},{51,3},{52,4},{53,5},{54,6},{55,7},{56,8},{57... | collective-permute-start | bytes 589832 | tf_op jit(solution)/shard_map/ppermute | solution.py:55
  6.0 8.6 %collective-permute-start.7 = (bf16[96,1024]{1,0:T(8,128)(2,1)S(1)}, bf16[96,1024]{1,0:T(8,128)(2,1)S(1)}, u32[]{:S(2)}, u32[]{:S(2)}) collective-permute-start(bf16[96,1024]{1,0:T(8,128)(2,1)S(1)} %get-tuple-element.13), channel_id=1, source_target_pairs={{32,0},{33,1},{34,2},{35,3},{36,4},{37,5},{38,6},{39,7},{40,8},{41... | collective-permute-start | bytes 589832 | tf_op jit(solution)/shard_map/ppermute | solution.py:55
  8.4 9.3 %collective-permute-start.8 = (bf16[96,1024]{1,0:T(8,128)(2,1)S(1)}, bf16[96,1024]{1,0:T(8,128)(2,1)S(1)}, u32[]{:S(2)}, u32[]{:S(2)}) collective-permute-start(bf16[96,1024]{1,0:T(8,128)(2,1)S(1)} %get-tuple-element.12), channel_id=1, source_target_pairs={{16,0},{17,1},{18,2},{19,3},{20,4},{21,5},{22,6},{23,7},{24,8},{25... | collective-permute-start | bytes 589832 | tf_op jit(solution)/shard_map/ppermute | solution.py:55
  9.7 9.5 %collective-permute-start = (bf16[96,1024]{1,0:T(8,128)(2,1)S(1)}, bf16[96,1024]{1,0:T(8,128)(2,1)S(1)}, u32[]{:S(2)}, u32[]{:S(2)}) collective-permute-start(bf16[96,1024]{1,0:T(8,128)(2,1)S(1)} %get-tuple-element.18), channel_id=1, source_target_pairs={{64,0},{65,1},{66,2},{67,3},{68,4},{69,5},{70,6},{71,7},{72,8},{73... | collective-permute-start | bytes 589832 | tf_op jit(solution)/shard_map/ppermute | solution.py:55
  12.1 7.7 %collective-permute-start.1 = (bf16[96,1024]{1,0:T(8,128)(2,1)S(1)}, bf16[96,1024]{1,0:T(8,128)(2,1)S(1)}, u32[]{:S(2)}, u32[]{:S(2)}) collective-permute-start(bf16[96,1024]{1,0:T(8,128)(2,1)S(1)} %get-tuple-element.17), channel_id=1, source_target_pairs={{112,0},{113,1},{114,2},{115,3},{116,4},{117,5},{118,6},{119,7},{1... | collective-permute-start | bytes 589832 | tf_op jit(solution)/shard_map/ppermute | solution.py:55
  12.8 8.7 %collective-permute-start.2 = (bf16[96,1024]{1,0:T(8,128)(2,1)S(1)}, bf16[96,1024]{1,0:T(8,128)(2,1)S(1)}, u32[]{:S(2)}, u32[]{:S(2)}) collective-permute-start(bf16[96,1024]{1,0:T(8,128)(2,1)S(1)} %get-tuple-element.16), channel_id=1, source_target_pairs={{96,0},{97,1},{98,2},{99,3},{100,4},{101,5},{102,6},{103,7},{104,8... | collective-permute-start | bytes 589832 | tf_op jit(solution)/shard_map/ppermute | solution.py:55
  14.6 7.7 %collective-permute-start.3 = (bf16[96,1024]{1,0:T(8,128)(2,1)S(1)}, bf16[96,1024]{1,0:T(8,128)(2,1)S(1)}, u32[]{:S(2)}, u32[]{:S(2)}) collective-permute-start(bf16[96,1024]{1,0:T(8,128)(2,1)S(1)} %get-tuple-element.15), channel_id=1, source_target_pairs={{80,0},{81,1},{82,2},{83,3},{84,4},{85,5},{86,6},{87,7},{88,8},{89... | collective-permute-start | bytes 589832 | tf_op jit(solution)/shard_map/ppermute | solution.py:55
  17.8 12.5 %collective-permute-start.14 = (bf16[384,1024]{1,0:T(8,128)(2,1)S(1)}, bf16[384,1024]{1,0:T(8,128)(2,1)S(1)}, u32[]{:S(2)}, u32[]{:S(2)}) collective-permute-start(bf16[384,1024]{1,0:T(8,128)(2,1)S(1)} %pad_maximum_fusion.refs_0_.refs_1_), channel_id=1, source_target_pairs={{4,0},{5,1},{6,2},{7,3},{8,4},{9,5},{10,6},{11,7},{12,8},{13,9},{1... | collective-permute-start | bytes 2359304 | tf_op jit(solution)/shard_map/ppermute | solution.py:55
  19.2 12.4 %collective-permute-start.9 = (bf16[384,1024]{1,0:T(8,128)(2,1)S(1)}, bf16[384,1024]{1,0:T(8,128)(2,1)S(1)}, u32[]{:S(2)}, u32[]{:S(2)}) collective-permute-start(bf16[384,1024]{1,0:T(8,128)(2,1)S(1)} %pad_maximum_fusion.refs_0_.refs_1_), channel_id=1, source_target_pairs={{1,0},{2,1},{3,2},{0,3},{5,4},{6,5},{7,6},{4,7},{9,8},{10,9},{11,1... | collective-permute-start | bytes 2359304 | tf_op jit(solution)/shard_map/ppermute | solution.py:55
  19.8 12.4 %collective-permute-start.11 = (bf16[384,1024]{1,0:T(8,128)(2,1)S(1)}, bf16[384,1024]{1,0:T(8,128)(2,1)S(1)}, u32[]{:S(2)}, u32[]{:S(2)}) collective-permute-start(bf16[384,1024]{1,0:T(8,128)(2,1)S(1)} %pad_maximum_fusion.refs_0_.refs_1_), channel_id=1, source_target_pairs={{3,0},{0,1},{1,2},{2,3},{7,4},{4,5},{5,6},{6,7},{11,8},{8,9},{9,10... | collective-permute-start | bytes 2359304 | tf_op jit(solution)/shard_map/ppermute | solution.py:55
  22.3 16.5 %collective-permute-start.10 = (bf16[384,1024]{1,0:T(8,128)(2,1)S(1)}, bf16[384,1024]{1,0:T(8,128)(2,1)S(1)}, u32[]{:S(2)}, u32[]{:S(2)}) collective-permute-start(bf16[384,1024]{1,0:T(8,128)(2,1)S(1)} %constant_dynamic-update-slice_fusion.refs_1_.refs_2_), channel_id=1, source_target_pairs={{1,0},{2,1},{3,2},{0,3},{5,4},{6,5},{7,6},{4,7},{9,8},{10,9},{11,1... | collective-permute-start | bytes 2359304 | tf_op jit(solution)/shard_map/ppermute | solution.py:55
  23.9 16.7 %collective-permute-start.4 = (bf16[384,1024]{1,0:T(8,128)(2,1)S(1)}, bf16[384,1024]{1,0:T(8,128)(2,1)S(1)}, u32[]{:S(2)}, u32[]{:S(2)}) collective-permute-start(bf16[384,1024]{1,0:T(8,128)(2,1)S(1)} %constant_dynamic-update-slice_fusion.refs_1_.refs_2_), channel_id=1, source_target_pairs={{4,0},{5,1},{6,2},{7,3},{8,4},{9,5},{10,6},{11,7},{12,8},{13,9},{1... | collective-permute-start | bytes 2359304 | tf_op jit(solution)/shard_map/ppermute | solution.py:55
  30.3 14.3 %collective-permute-start.16 = (bf16[384,1024]{1,0:T(8,128)(2,1)S(1)}, bf16[384,1024]{1,0:T(8,128)(2,1)S(1)}, u32[]{:S(2)}, u32[]{:S(2)}) collective-permute-start(bf16[384,1024]{1,0:T(8,128)(2,1)S(1)} %constant_dynamic-update-slice_fusion.refs_1_.refs_2_), channel_id=1, source_target_pairs={{3,0},{0,1},{1,2},{2,3},{7,4},{4,5},{5,6},{6,7},{11,8},{8,9},{9,10... | collective-permute-start | bytes 2359304 | tf_op jit(solution)/shard_map/ppermute | solution.py:55
  31.6 16.0 %collective-permute-start.15 = (bf16[384,1024]{1,0:T(8,128)(2,1)S(1)}, bf16[384,1024]{1,0:T(8,128)(2,1)S(1)}, u32[]{:S(2)}, u32[]{:S(2)}) collective-permute-start(bf16[384,1024]{1,0:T(8,128)(2,1)S(1)} %collective-permute-done.14.refs_0_.refs_2_.refs_3_), channel_id=1, source_target_pairs={{4,0},{5,1},{6,2},{7,3},{8,4},{9,5},{10,6},{11,7},{12,8},{13,9},{1... | collective-permute-start | bytes 2359304 | tf_op jit(solution)/shard_map/ppermute | solution.py:55
  32.2 18.8 %collective-permute-start.12 = (bf16[384,1024]{1,0:T(8,128)(2,1)S(1)}, bf16[384,1024]{1,0:T(8,128)(2,1)S(1)}, u32[]{:S(2)}, u32[]{:S(2)}) collective-permute-start(bf16[384,1024]{1,0:T(8,128)(2,1)S(1)} %collective-permute-done.11.refs_4_), channel_id=1, source_target_pairs={{3,0},{0,1},{1,2},{2,3},{7,4},{4,5},{5,6},{6,7},{11,8},{8,9},{9,10... | collective-permute-start | bytes 2359304 | tf_op jit(solution)/shard_map/ppermute | solution.py:55
  38.8 13.7 %collective-permute-start.13 = (bf16[384,1024]{1,0:T(8,128)(2,1)S(1)}, bf16[384,1024]{1,0:T(8,128)(2,1)S(1)}, u32[]{:S(2)}, u32[]{:S(2)}) collective-permute-start(bf16[384,1024]{1,0:T(8,128)(2,1)S(1)} %collective-permute-done.10.refs_3_.refs_1_.refs_4_), channel_id=1, source_target_pairs={{1,0},{2,1},{3,2},{0,3},{5,4},{6,5},{7,6},{4,7},{9,8},{10,9},{11,1... | collective-permute-start | bytes 2359304 | tf_op jit(solution)/shard_map/ppermute | solution.py:55
  40.7 14.6 %collective-permute-start.5 = (bf16[384,1024]{1,0:T(8,128)(2,1)S(1)}, bf16[384,1024]{1,0:T(8,128)(2,1)S(1)}, u32[]{:S(2)}, u32[]{:S(2)}) collective-permute-start(bf16[384,1024]{1,0:T(8,128)(2,1)S(1)} %collective-permute-done.4.refs_0_.refs_3_.refs_4_), channel_id=1, source_target_pairs={{4,0},{5,1},{6,2},{7,3},{8,4},{9,5},{10,6},{11,7},{12,8},{13,9},{1... | collective-permute-start | bytes 2359304 | tf_op jit(solution)/shard_map/ppermute | solution.py:55
where the time goes:
time: 78 us; the launch traced here: 77.8 us
  starting transfers between devices  23.5 us (30%)
  Pallas kernels  19.3 us (25%)
  blocking collectives  18.1 us (23%)
  waiting for transfers between devices  14.6 us (19%)
  local copies, waits for them, and re-layouts  2.07 us (3%)
    ppermute x17, starting transfers between devices, take(): return lax.ppermute(block, AXES, route)  23.5 us
    all_to_all x1, blocking collectives, on_device(): got = lax.all_to_all(best, AXES, 0, 0, tiled=True)  18.1 us
    pallas_call x9, Pallas kernels, pair_max(): pl.pallas_call(functools.partial(pair_kernel, names, blocks, products), i...  15.5 us
    ppermute x17, waiting for transfers between devices, take(): return lax.ppermute(block, AXES, route)  14.6 us
    unnamed x9, local copies, waits for them, and re-layouts  1.95 us
    pallas_call x1, Pallas kernels, sort_rows(): pl.pallas_call(sort_kernel, in_specs=[hbm, hbm], out_specs=[vmem] * 3, ou...  1.89 us
    pallas_call x1, Pallas kernels, unsort(): pl.pallas_call(unsort_kernel, in_specs=[vmem] * 2, out_specs=vmem, out_sh...  1.84 us
  transfers between devices with their start and end apart: 17, of which 7 were waited for; matrix products, arithmetic and copies ran while one was open for 0% of the time, Pallas kernels for 17%

commit v1 on v0

--- a/solution.py
+++ b/solution.py
@@ -27,7 +27,6 @@
 BLOCKS = tuple(STEPS)
 SECTIONS = 2 * SIDE
 LANES = 128
-CHUNKS = 4
 EFFORT = 6
 LOW = -8.0
 NONE = -2.0
@@ -67,25 +66,14 @@
     return ring * jnp.where(core == 0, 16, 1) + u * jnp.where(core == 0, 1, 16) + y * 4
 
 
-def sort_kernel(rows_hbm, cluster_hbm, mine_ref, other_ref, slot_ref, *scratch):
-    rows_ref, cluster_ref, normed_ref, sems = scratch
+def sort_kernel(rows_ref, cluster_ref, mine_ref, other_ref, slot_ref):
     rows = rows_ref.shape[0]
-    step = rows // CHUNKS
-    copies = [pltpu.make_async_copy(cluster_hbm, cluster_ref, sems.at[CHUNKS])]
-    for k in range(CHUNKS):
-        part = pl.ds(k * step, step)
-        copies.append(
-            pltpu.make_async_copy(rows_hbm.at[part, :], rows_ref.at[part, :], sems.at[k])
-        )
-    for copy in copies:
-        copy.start()
     core, z, y, x = here()
     ring_mine, ring_other = jnp.where(core == 0, z, x), jnp.where(core == 0, x, z)
     before = lax.broadcasted_iota(jnp.int32, (rows, rows), 0) < lax.broadcasted_iota(
         jnp.int32, (rows, rows), 1
     )
     before = jnp.where(before, 1.0, 0.0).astype(jnp.bfloat16)
-    copies[0].wait()
     cluster = cluster_ref[...]
     hits = cluster == lax.broadcasted_iota(jnp.int32, (8, rows), 0)
     hits = jnp.where(hits, 1.0, 0.0)
@@ -95,13 +83,9 @@
     turn = (cluster + 4 - jnp.where(is_mine, ring_mine, ring_other)) % 4
     slot = (jnp.where(is_mine, 0, 4) + turn) * BOUND + rank
     slot_ref[...] = slot
-    for k in range(CHUNKS):
-        copies[1 + k].wait()
-        part = slice(k * step, (k + 1) * step)
-        values = rows_ref[part, :].astype(jnp.float32)
-        total = jnp.sum(values * values, 1, keepdims=True)
-        normed_ref[part, :] = (values * lax.rsqrt(total + 1e-06)).astype(jnp.bfloat16)
-    normed = normed_ref[...]
+    values = rows_ref[...].astype(jnp.float32)
+    total = jnp.sum(values * values, 1, keepdims=True)
+    normed = (values * lax.rsqrt(total + 1e-06)).astype(jnp.bfloat16)
     for start, out_ref in ((0, mine_ref), (HALF, other_ref)):
         picks = slot - start == lax.broadcasted_iota(jnp.int32, (HALF, rows), 0)
         picks = jnp.where(picks, 1.0, 0.0)
@@ -116,21 +100,14 @@
 def sort_rows(embeddings, cluster):
     rows, width = embeddings.shape
     vmem = pl.BlockSpec(memory_space=pltpu.VMEM)
-    hbm = pl.BlockSpec(memory_space=pltpu.HBM)
     return pl.pallas_call(
         sort_kernel,
-        in_specs=[hbm, hbm],
+        in_specs=[vmem, vmem],
         out_specs=[vmem] * 3,
         out_shape=[
             jax.ShapeDtypeStruct((HALF, width), jnp.bfloat16),
             jax.ShapeDtypeStruct((HALF, width), jnp.bfloat16),
             jax.ShapeDtypeStruct((1, rows), jnp.int32),
-        ],
-        scratch_shapes=[
-            pltpu.VMEM((rows, width), jnp.bfloat16),
-            pltpu.VMEM((1, rows), jnp.int32),
-            pltpu.VMEM((rows, width), jnp.bfloat16),
-            pltpu.SemaphoreType.DMA((CHUNKS + 1,)),
         ],
         compiler_params=pltpu.CompilerParams(vmem_limit_bytes=20 << 20),
         cost_estimate=pl.CostEstimate(

time: 78 us -> 77.5 us (level)
  no operation moved by 1% of the time
where the time goes in v1:
time: 77.5 us; the launch traced here: 77.3 us
  starting transfers between devices  23.5 us (30%)
  Pallas kernels  18.8 us (24%)
  blocking collectives  18.1 us (23%)
  waiting for transfers between devices  14.6 us (19%)
  local copies, waits for them, and re-layouts  2.07 us (3%)
    ppermute x17, starting transfers between devices, take(): return lax.ppermute(block, AXES, route)  23.5 us
    all_to_all x1, blocking collectives, on_device(): got = lax.all_to_all(best, AXES, 0, 0, tiled=True)  18.1 us
    pallas_call x9, Pallas kernels, pair_max(): pl.pallas_call(functools.partial(pair_kernel, names, blocks, products), i...  15.5 us
    ppermute x17, waiting for transfers between devices, take(): return lax.ppermute(block, AXES, route)  14.6 us
    unnamed x9, local copies, waits for them, and re-layouts  1.95 us
    pallas_call x1, Pallas kernels, unsort(): pl.pallas_call(unsort_kernel, in_specs=[vmem] * 2, out_specs=vmem, out_sh...  1.84 us
  transfers between devices with their start and end apart: 17, of which 7 were waited for; matrix products, arithmetic and copies ran while one was open for 0% of the time, Pallas kernels for 17%

profile of v1, /device:TPU:1, one launch (start us, length us, event | category | flops | bytes accessed | tf_op | source)
XLA Modules:
  0.0 77.3 jit_solution(10371204278792582487)
XLA Ops:
  0.0 1.2 %copy-done.1 = bf16[512,1024]{1,0:T(8,128)(2,1)S(1)} copy-done((bf16[512,1024]{1,0:T(8,128)(2,1)S(1)}, bf16[512,1024]{1,0:T(8,128)(2,1)}, u32[]{:S(2)}) %copy-start.1) | copy-done | bytes 1048600
  1.2 0.7 copy-done.2
  1.9 1.4 %sort_rows.1 = (bf16[384,1024]{1,0:T(8,128)(2,1)S(1)}, bf16[384,1024]{1,0:T(8,128)(2,1)S(1)}, s32[1,512]{1,0:T(1,128)S(1)}) custom-call(bf16[512,1024]{1,0:T(8,128)(2,1)S(1)} %copy-done.1, s32[1,512]{1,0:T(1,128)S(1)} %bitcast.7), custom_call_target="tpu_custom_call" | custom-call | flops 805306368 | bytes 3145728 | tf_op jit(solution)/shard_map/sort_rows/pallas_call | solution.py:103
  3.3 0.1 fusion
  3.4 2.1 %collective-permute-start.6 = (bf16[96,1024]{1,0:T(8,128)(2,1)S(1)}, bf16[96,1024]{1,0:T(8,128)(2,1)S(1)}, u32[]{:S(2)}, u32[]{:S(2)}) collective-permute-start(bf16[96,1024]{1,0:T(8,128)(2,1)S(1)} %get-tuple-element.14), channel_id=1, source_target_pairs={{48,0},{49,1},{50,2},{51,3},{52,4},{53,5},{54,6},{55,7},{56,8},{57... | collective-permute-start | bytes 589832 | tf_op jit(solution)/shard_map/ppermute | solution.py:54
  5.5 2.5 %collective-permute-start.7 = (bf16[96,1024]{1,0:T(8,128)(2,1)S(1)}, bf16[96,1024]{1,0:T(8,128)(2,1)S(1)}, u32[]{:S(2)}, u32[]{:S(2)}) collective-permute-start(bf16[96,1024]{1,0:T(8,128)(2,1)S(1)} %get-tuple-element.13), channel_id=1, source_target_pairs={{32,0},{33,1},{34,2},{35,3},{36,4},{37,5},{38,6},{39,7},{40,8},{41... | collective-permute-start | bytes 589832 | tf_op jit(solution)/shard_map/ppermute | solution.py:54
  7.9 1.2 %collective-permute-start.8 = (bf16[96,1024]{1,0:T(8,128)(2,1)S(1)}, bf16[96,1024]{1,0:T(8,128)(2,1)S(1)}, u32[]{:S(2)}, u32[]{:S(2)}) collective-permute-start(bf16[96,1024]{1,0:T(8,128)(2,1)S(1)} %get-tuple-element.12), channel_id=1, source_target_pairs={{16,0},{17,1},{18,2},{19,3},{20,4},{21,5},{22,6},{23,7},{24,8},{25... | collective-permute-start | bytes 589832 | tf_op jit(solution)/shard_map/ppermute | solution.py:54
  9.1 0.1 fusion.1
  9.2 2.5 %collective-permute-start = (bf16[96,1024]{1,0:T(8,128)(2,1)S(1)}, bf16[96,1024]{1,0:T(8,128)(2,1)S(1)}, u32[]{:S(2)}, u32[]{:S(2)}) collective-permute-start(bf16[96,1024]{1,0:T(8,128)(2,1)S(1)} %get-tuple-element.18), channel_id=1, source_target_pairs={{64,0},{65,1},{66,2},{67,3},{68,4},{69,5},{70,6},{71,7},{72,8},{73... | collective-permute-start | bytes 589832 | tf_op jit(solution)/shard_map/ppermute | solution.py:54
  11.6 0.7 collective-permute-start.1
  12.3 0.0 collective-permute-done.6
  12.3 1.8 %collective-permute-start.2 = (bf16[96,1024]{1,0:T(8,128)(2,1)S(1)}, bf16[96,1024]{1,0:T(8,128)(2,1)S(1)}, u32[]{:S(2)}, u32[]{:S(2)}) collective-permute-start(bf16[96,1024]{1,0:T(8,128)(2,1)S(1)} %get-tuple-element.16), channel_id=1, source_target_pairs={{96,0},{97,1},{98,2},{99,3},{100,4},{101,5},{102,6},{103,7},{104,8... | collective-permute-start | bytes 589832 | tf_op jit(solution)/shard_map/ppermute | solution.py:54
  14.1 0.0 collective-permute-done.7
  14.1 3.2 %collective-permute-start.3 = (bf16[96,1024]{1,0:T(8,128)(2,1)S(1)}, bf16[96,1024]{1,0:T(8,128)(2,1)S(1)}, u32[]{:S(2)}, u32[]{:S(2)}) collective-permute-start(bf16[96,1024]{1,0:T(8,128)(2,1)S(1)} %get-tuple-element.15), channel_id=1, source_target_pairs={{80,0},{81,1},{82,2},{83,3},{84,4},{85,5},{86,6},{87,7},{88,8},{89... | collective-permute-start | bytes 589832 | tf_op jit(solution)/shard_map/ppermute | solution.py:54
  17.3 0.0 collective-permute-done.8
  17.3 0.1 pad_maximum_fusion.refs_0_.refs_1_
  17.3 1.4 %collective-permute-start.14 = (bf16[384,1024]{1,0:T(8,128)(2,1)S(1)}, bf16[384,1024]{1,0:T(8,128)(2,1)S(1)}, u32[]{:S(2)}, u32[]{:S(2)}) collective-permute-start(bf16[384,1024]{1,0:T(8,128)(2,1)S(1)} %pad_maximum_fusion.refs_0_.refs_1_), channel_id=1, source_target_pairs={{4,0},{5,1},{6,2},{7,3},{8,4},{9,5},{10,6},{11,7},{12,8},{13,9},{1... | collective-permute-start | bytes 2359304 | tf_op jit(solution)/shard_map/ppermute | solution.py:54
  18.7 0.0 collective-permute-done
  18.7 0.6 collective-permute-start.9
  19.3 0.0 collective-permute-done.1
  19.3 0.9 %collective-permute-start.11 = (bf16[384,1024]{1,0:T(8,128)(2,1)S(1)}, bf16[384,1024]{1,0:T(8,128)(2,1)S(1)}, u32[]{:S(2)}, u32[]{:S(2)}) collective-permute-start(bf16[384,1024]{1,0:T(8,128)(2,1)S(1)} %pad_maximum_fusion.refs_0_.refs_1_), channel_id=1, source_target_pairs={{3,0},{0,1},{1,2},{2,3},{7,4},{4,5},{5,6},{6,7},{11,8},{8,9},{9,10... | collective-permute-start | bytes 2359304 | tf_op jit(solution)/shard_map/ppermute | solution.py:54
  20.3 0.7 collective-permute-done.2
  21.0 0.7 collective-permute-done.3
  21.8 1.6 %collective-permute-start.10 = (bf16[384,1024]{1,0:T(8,128)(2,1)S(1)}, bf16[384,1024]{1,0:T(8,128)(2,1)S(1)}, u32[]{:S(2)}, u32[]{:S(2)}) collective-permute-start(bf16[384,1024]{1,0:T(8,128)(2,1)S(1)} %constant_dynamic-update-slice_fusion.refs_1_.refs_2_), channel_id=1, source_target_pairs={{1,0},{2,1},{3,2},{0,3},{5,4},{6,5},{7,6},{4,7},{9,8},{10,9},{11,1... | collective-permute-start | bytes 2359304 | tf_op jit(solution)/shard_map/ppermute | solution.py:54
  23.4 1.3 %collective-permute-start.4 = (bf16[384,1024]{1,0:T(8,128)(2,1)S(1)}, bf16[384,1024]{1,0:T(8,128)(2,1)S(1)}, u32[]{:S(2)}, u32[]{:S(2)}) collective-permute-start(bf16[384,1024]{1,0:T(8,128)(2,1)S(1)} %constant_dynamic-update-slice_fusion.refs_1_.refs_2_), channel_id=1, source_target_pairs={{4,0},{5,1},{6,2},{7,3},{8,4},{9,5},{10,6},{11,7},{12,8},{13,9},{1... | collective-permute-start | bytes 2359304 | tf_op jit(solution)/shard_map/ppermute | solution.py:54
  24.7 1.5 %pair_max.9.refs_3_ = f32[6,768]{1,0:T(8,128)S(1)} custom-call(bf16[384,1024]{1,0:T(8,128)(2,1)S(1)} %pad_maximum_fusion.refs_0_.refs_1_, bf16[384,1024]{1,0:T(8,128)(2,1)S(1)} %constant_dynamic-update-slice_fusion.refs_1_.refs_2_, f32[6,768]{1,0:T(8,128)S(1)} %broadcast_in_dim.3.refs_2_), custom_call_target="tpu_custom_call" | custom-call | flops 7247757312 | bytes 1572864 | tf_op jit(solution)/shard_map/pair_max/pallas_call | solution.py:201
  26.2 3.6 %collective-permute-done.14.refs_0_.refs_2_.refs_3_ = bf16[384,1024]{1,0:T(8,128)(2,1)S(1)} collective-permute-done((bf16[384,1024]{1,0:T(8,128)(2,1)S(1)}, bf16[384,1024]{1,0:T(8,128)(2,1)S(1)}, u32[]{:S(2)}, u32[]{:S(2)}) %collective-permute-start.14) | collective-permute-done | bytes 786464 | tf_op jit(solution)/shard_map/ppermute | solution.py:54
  29.8 0.3 collective-permute-start.16
  30.1 1.0 %pair_max.10.refs_3_ = f32[6,768]{1,0:T(8,128)S(1)} custom-call(bf16[384,1024]{1,0:T(8,128)(2,1)S(1)} %collective-permute-done.14.refs_0_.refs_2_.refs_3_, bf16[384,1024]{1,0:T(8,128)(2,1)S(1)} %pad_maximum_fusion.refs_0_.refs_1_, bf16[384,1024]{1,0:T(8,128)(2,1)S(1)} %constant_dynamic-update-slice_fusion.refs_1_.refs_2_, f32[6,768]{1,0:T(8,128)S(1)} %pair_max.9.refs_3_), custom_call_target="tpu_custom_call" | custom-call | flops 3623878656 | bytes 2359296 | tf_op jit(solution)/shard_map/pair_max/pallas_call | solution.py:201
  31.1 0.1 collective-permute-start.15
  31.2 0.5 collective-permute-done.11.refs_4_
  31.8 0.2 collective-permute-start.12
  32.0 6.3 %collective-permute-done.10.refs_3_.refs_1_.refs_4_ = bf16[384,1024]{1,0:T(8,128)(2,1)S(1)} collective-permute-done((bf16[384,1024]{1,0:T(8,128)(2,1)S(1)}, bf16[384,1024]{1,0:T(8,128)(2,1)S(1)}, u32[]{:S(2)}, u32[]{:S(2)}) %collective-permute-start.10) | collective-permute-done | bytes 786464 | tf_op jit(solution)/shard_map/ppermute | solution.py:54
  38.3 1.9 %collective-permute-start.13 = (bf16[384,1024]{1,0:T(8,128)(2,1)S(1)}, bf16[384,1024]{1,0:T(8,128)(2,1)S(1)}, u32[]{:S(2)}, u32[]{:S(2)}) collective-permute-start(bf16[384,1024]{1,0:T(8,128)(2,1)S(1)} %collective-permute-done.10.refs_3_.refs_1_.refs_4_), channel_id=1, source_target_pairs={{1,0},{2,1},{3,2},{0,3},{5,4},{6,5},{7,6},{4,7},{9,8},{10,9},{11,1... | collective-permute-start | bytes 2359304 | tf_op jit(solution)/shard_map/ppermute | solution.py:54
  40.2 0.0 collective-permute-done.4.refs_0_.refs_3_.refs_4_
  40.2 1.3 %collective-permute-start.5 = (bf16[384,1024]{1,0:T(8,128)(2,1)S(1)}, bf16[384,1024]{1,0:T(8,128)(2,1)S(1)}, u32[]{:S(2)}, u32[]{:S(2)}) collective-permute-start(bf16[384,1024]{1,0:T(8,128)(2,1)S(1)} %collective-permute-done.4.refs_0_.refs_3_.refs_4_), channel_id=1, source_target_pairs={{4,0},{5,1},{6,2},{7,3},{8,4},{9,5},{10,6},{11,7},{12,8},{13,9},{1... | collective-permute-start | bytes 2359304 | tf_op jit(solution)/shard_map/ppermute | solution.py:54
  41.5 1.0 %pair_max.11.refs_4_ = f32[6,768]{1,0:T(8,128)S(1)} custom-call(bf16[384,1024]{1,0:T(8,128)(2,1)S(1)} %collective-permute-done.9.refs_0_.refs_3_, bf16[384,1024]{1,0:T(8,128)(2,1)S(1)} %pad_maximum_fusion.refs_0_.refs_1_, bf16[384,1024]{1,0:T(8,128)(2,1)S(1)} %constant_dynamic-update-slice_fusion.refs_1_.refs_2_, f32[6,768]{1,0:T(8,128)S(1)} %pair_max.10.refs_3_, ...), custom_call_target="tpu_custom_call" | custom-call | flops 3623878656 | bytes 2359296 | tf_op jit(solution)/shard_map/pair_max/pallas_call | solution.py:201
  42.4 1.6 %pair_max.12.refs_6_ = f32[6,768]{1,0:T(8,128)S(1)} custom-call(bf16[384,1024]{1,0:T(8,128)(2,1)S(1)} %collective-permute-done.4.refs_0_.refs_3_.refs_4_, bf16[384,1024]{1,0:T(8,128)(2,1)S(1)} %pad_maximum_fusion.refs_0_.refs_1_, bf16[384,1024]{1,0:T(8,128)(2,1)S(1)} %constant_dynamic-update-slice_fusion.refs_1_.refs_2_, ...), custom_call_target="tpu_custom_call" | custom-call | flops 7247757312 | bytes 3145728 | tf_op jit(solution)/shard_map/pair_max/pallas_call | solution.py:201
  44.1 0.0 collective-permute-done.16.refs_5_
  44.1 3.1 %pair_max.13.refs_5_ = f32[6,768]{1,0:T(8,128)S(1)} custom-call(bf16[384,1024]{1,0:T(8,128)(2,1)S(1)} %collective-permute-done.9.refs_0_.refs_3_, bf16[384,1024]{1,0:T(8,128)(2,1)S(1)} %collective-permute-done.10.refs_3_.refs_1_.refs_4_, bf16[384,1024]{1,0:T(8,128)(2,1)S(1)} %collective-permute-done.14.refs_0_.refs_2_.refs_3_, ...), custom_call_target="tpu_custom_call" | custom-call | flops 14495514624 | bytes 4718592 | tf_op jit(solution)/shard_map/pair_max/pallas_call | solution.py:201
  47.2 1.5 %pair_max.14.refs_5_ = f32[6,768]{1,0:T(8,128)S(1)} custom-call(bf16[384,1024]{1,0:T(8,128)(2,1)S(1)} %collective-permute-done.15.refs_0_.refs_5_, bf16[384,1024]{1,0:T(8,128)(2,1)S(1)} %pad_maximum_fusion.refs_0_.refs_1_, bf16[384,1024]{1,0:T(8,128)(2,1)S(1)} %constant_dynamic-update-slice_fusion.refs_1_.refs_2_, ...), custom_call_target="tpu_custom_call" | custom-call | flops 6039797760 | bytes 3932160 | tf_op jit(solution)/shard_map/pair_max/pallas_call | solution.py:201
  48.6 2.0 %collective-permute-done.12.refs_0_.refs_6_.refs_5_ = bf16[384,1024]{1,0:T(8,128)(2,1)S(1)} collective-permute-done((bf16[384,1024]{1,0:T(8,128)(2,1)S(1)}, bf16[384,1024]{1,0:T(8,128)(2,1)S(1)}, u32[]{:S(2)}, u32[]{:S(2)}) %collective-permute-start.12) | collective-permute-done | bytes 786464 | tf_op jit(solution)/shard_map/ppermute | solution.py:54
  50.6 1.4 %pair_max.15.refs_7_ = f32[6,768]{1,0:T(8,128)S(1)} custom-call(bf16[384,1024]{1,0:T(8,128)(2,1)S(1)} %collective-permute-done.12.refs_0_.refs_6_.refs_5_, bf16[384,1024]{1,0:T(8,128)(2,1)S(1)} %pad_maximum_fusion.refs_0_.refs_1_, bf16[384,1024]{1,0:T(8,128)(2,1)S(1)} %constant_dynamic-update-slice_fusion.refs_1_.refs_2_, ...), custom_call_target="tpu_custom_call" | custom-call | flops 6039797760 | bytes 3932160 | tf_op jit(solution)/shard_map/pair_max/pallas_call | solution.py:201
  52.0 2.1 %pair_max.16.refs_7_ = f32[6,768]{1,0:T(8,128)S(1)} custom-call(bf16[384,1024]{1,0:T(8,128)(2,1)S(1)} %collective-permute-done.13.refs_0_.refs_6_, bf16[384,1024]{1,0:T(8,128)(2,1)S(1)} %pad_maximum_fusion.refs_0_.refs_1_, bf16[384,1024]{1,0:T(8,128)(2,1)S(1)} %constant_dynamic-update-slice_fusion.refs_1_.refs_2_, ...), custom_call_target="tpu_custom_call" | custom-call | flops 9663676416 | bytes 5505024 | tf_op jit(solution)/shard_map/pair_max/pallas_call | solution.py:201
  54.1 0.7 collective-permute-done.5.refs_0_
  54.8 2.5 %pair_max.17 = f32[128,128]{1,0:T(8,128)S(1)} custom-call(bf16[384,1024]{1,0:T(8,128)(2,1)S(1)} %collective-permute-done.5.refs_0_, bf16[384,1024]{1,0:T(8,128)(2,1)S(1)} %pad_maximum_fusion.refs_0_.refs_1_, bf16[384,1024]{1,0:T(8,128)(2,1)S(1)} %constant_dynamic-update-slice_fusion.refs_1_.refs_2_, ...), custom_call_target="tpu_custom_call" | custom-call | flops 10871635968 | bytes 5505024 | tf_op jit(solution)/shard_map/pair_max/pallas_call | solution.py:201
  57.3 18.1 %all_to_all.11 = f32[128,1,128]{2,1,0:T(1,128)} all-to-all(f32[128,1,128]{2,1,0:T(1,128)S(1)} %bitcast.6), channel_id=1, replica_groups=mesh['group'=2,'member'=64] {'group','member'}, dimensions={0} | all-to-all | bytes 131072 | tf_op jit(solution)/shard_map/all_to_all | solution.py:296
  75.4 1.8 %unsort.1 = f32[1,512]{1,0:T(1,128)} custom-call(f32[128,128]{1,0:T(8,128)} %bitcast.8, s32[1,512]{1,0:T(1,128)} %copy-done), custom_call_target="tpu_custom_call" | custom-call | tf_op jit(solution)/shard_map/unsort/pallas_call | solution.py:244
  (12 shorter events, 0.1 us)
Async XLA Ops:
  0.0 1.2 %copy-start.1 = (bf16[512,1024]{1,0:T(8,128)(2,1)S(1)}, bf16[512,1024]{1,0:T(8,128)(2,1)}, u32[]{:S(2)}) copy-start(bf16[512,1024]{1,0:T(8,128)(2,1)} %rows_ref.1) | copy-start | bytes 3145732
  1.2 0.7 copy-start.2
  3.3 5.8 %copy-start = (s32[1,512]{1,0:T(1,128)}, s32[1,512]{1,0:T(1,128)S(1)}, u32[]{:S(2)}) copy-start(s32[1,512]{1,0:T(1,128)S(1)} %get-tuple-element.10.slot_ref) | copy-start | bytes 6148
  3.4 8.9 %collective-permute-start.6 = (bf16[96,1024]{1,0:T(8,128)(2,1)S(1)}, bf16[96,1024]{1,0:T(8,128)(2,1)S(1)}, u32[]{:S(2)}, u32[]{:S(2)}) collective-permute-start(bf16[96,1024]{1,0:T(8,128)(2,1)S(1)} %get-tuple-element.14), channel_id=1, source_target_pairs={{48,0},{49,1},{50,2},{51,3},{52,4},{53,5},{54,6},{55,7},{56,8},{57... | collective-permute-start | bytes 589832 | tf_op jit(solution)/shard_map/ppermute | solution.py:54
  5.5 8.6 %collective-permute-start.7 = (bf16[96,1024]{1,0:T(8,128)(2,1)S(1)}, bf16[96,1024]{1,0:T(8,128)(2,1)S(1)}, u32[]{:S(2)}, u32[]{:S(2)}) collective-permute-start(bf16[96,1024]{1,0:T(8,128)(2,1)S(1)} %get-tuple-element.13), channel_id=1, source_target_pairs={{32,0},{33,1},{34,2},{35,3},{36,4},{37,5},{38,6},{39,7},{40,8},{41... | collective-permute-start | bytes 589832 | tf_op jit(solution)/shard_map/ppermute | solution.py:54
  7.9 9.3 %collective-permute-start.8 = (bf16[96,1024]{1,0:T(8,128)(2,1)S(1)}, bf16[96,1024]{1,0:T(8,128)(2,1)S(1)}, u32[]{:S(2)}, u32[]{:S(2)}) collective-permute-start(bf16[96,1024]{1,0:T(8,128)(2,1)S(1)} %get-tuple-element.12), channel_id=1, source_target_pairs={{16,0},{17,1},{18,2},{19,3},{20,4},{21,5},{22,6},{23,7},{24,8},{25... | collective-permute-start | bytes 589832 | tf_op jit(solution)/shard_map/ppermute | solution.py:54
  9.2 9.6 %collective-permute-start = (bf16[96,1024]{1,0:T(8,128)(2,1)S(1)}, bf16[96,1024]{1,0:T(8,128)(2,1)S(1)}, u32[]{:S(2)}, u32[]{:S(2)}) collective-permute-start(bf16[96,1024]{1,0:T(8,128)(2,1)S(1)} %get-tuple-element.18), channel_id=1, source_target_pairs={{64,0},{65,1},{66,2},{67,3},{68,4},{69,5},{70,6},{71,7},{72,8},{73... | collective-permute-start | bytes 589832 | tf_op jit(solution)/shard_map/ppermute | solution.py:54
  11.6 7.7 %collective-permute-start.1 = (bf16[96,1024]{1,0:T(8,128)(2,1)S(1)}, bf16[96,1024]{1,0:T(8,128)(2,1)S(1)}, u32[]{:S(2)}, u32[]{:S(2)}) collective-permute-start(bf16[96,1024]{1,0:T(8,128)(2,1)S(1)} %get-tuple-element.17), channel_id=1, source_target_pairs={{112,0},{113,1},{114,2},{115,3},{116,4},{117,5},{118,6},{119,7},{1... | collective-permute-start | bytes 589832 | tf_op jit(solution)/shard_map/ppermute | solution.py:54
  12.3 8.7 %collective-permute-start.2 = (bf16[96,1024]{1,0:T(8,128)(2,1)S(1)}, bf16[96,1024]{1,0:T(8,128)(2,1)S(1)}, u32[]{:S(2)}, u32[]{:S(2)}) collective-permute-start(bf16[96,1024]{1,0:T(8,128)(2,1)S(1)} %get-tuple-element.16), channel_id=1, source_target_pairs={{96,0},{97,1},{98,2},{99,3},{100,4},{101,5},{102,6},{103,7},{104,8... | collective-permute-start | bytes 589832 | tf_op jit(solution)/shard_map/ppermute | solution.py:54
  14.1 7.7 %collective-permute-start.3 = (bf16[96,1024]{1,0:T(8,128)(2,1)S(1)}, bf16[96,1024]{1,0:T(8,128)(2,1)S(1)}, u32[]{:S(2)}, u32[]{:S(2)}) collective-permute-start(bf16[96,1024]{1,0:T(8,128)(2,1)S(1)} %get-tuple-element.15), channel_id=1, source_target_pairs={{80,0},{81,1},{82,2},{83,3},{84,4},{85,5},{86,6},{87,7},{88,8},{89... | collective-permute-start | bytes 589832 | tf_op jit(solution)/shard_map/ppermute | solution.py:54
  17.3 12.5 %collective-permute-start.14 = (bf16[384,1024]{1,0:T(8,128)(2,1)S(1)}, bf16[384,1024]{1,0:T(8,128)(2,1)S(1)}, u32[]{:S(2)}, u32[]{:S(2)}) collective-permute-start(bf16[384,1024]{1,0:T(8,128)(2,1)S(1)} %pad_maximum_fusion.refs_0_.refs_1_), channel_id=1, source_target_pairs={{4,0},{5,1},{6,2},{7,3},{8,4},{9,5},{10,6},{11,7},{12,8},{13,9},{1... | collective-permute-start | bytes 2359304 | tf_op jit(solution)/shard_map/ppermute | solution.py:54
  18.7 12.4 %collective-permute-start.9 = (bf16[384,1024]{1,0:T(8,128)(2,1)S(1)}, bf16[384,1024]{1,0:T(8,128)(2,1)S(1)}, u32[]{:S(2)}, u32[]{:S(2)}) collective-permute-start(bf16[384,1024]{1,0:T(8,128)(2,1)S(1)} %pad_maximum_fusion.refs_0_.refs_1_), channel_id=1, source_target_pairs={{1,0},{2,1},{3,2},{0,3},{5,4},{6,5},{7,6},{4,7},{9,8},{10,9},{11,1... | collective-permute-start | bytes 2359304 | tf_op jit(solution)/shard_map/ppermute | solution.py:54
  19.3 12.4 %collective-permute-start.11 = (bf16[384,1024]{1,0:T(8,128)(2,1)S(1)}, bf16[384,1024]{1,0:T(8,128)(2,1)S(1)}, u32[]{:S(2)}, u32[]{:S(2)}) collective-permute-start(bf16[384,1024]{1,0:T(8,128)(2,1)S(1)} %pad_maximum_fusion.refs_0_.refs_1_), channel_id=1, source_target_pairs={{3,0},{0,1},{1,2},{2,3},{7,4},{4,5},{5,6},{6,7},{11,8},{8,9},{9,10... | collective-permute-start | bytes 2359304 | tf_op jit(solution)/shard_map/ppermute | solution.py:54
  21.8 16.5 %collective-permute-start.10 = (bf16[384,1024]{1,0:T(8,128)(2,1)S(1)}, bf16[384,1024]{1,0:T(8,128)(2,1)S(1)}, u32[]{:S(2)}, u32[]{:S(2)}) collective-permute-start(bf16[384,1024]{1,0:T(8,128)(2,1)S(1)} %constant_dynamic-update-slice_fusion.refs_1_.refs_2_), channel_id=1, source_target_pairs={{1,0},{2,1},{3,2},{0,3},{5,4},{6,5},{7,6},{4,7},{9,8},{10,9},{11,1... | collective-permute-start | bytes 2359304 | tf_op jit(solution)/shard_map/ppermute | solution.py:54
  23.4 16.7 %collective-permute-start.4 = (bf16[384,1024]{1,0:T(8,128)(2,1)S(1)}, bf16[384,1024]{1,0:T(8,128)(2,1)S(1)}, u32[]{:S(2)}, u32[]{:S(2)}) collective-permute-start(bf16[384,1024]{1,0:T(8,128)(2,1)S(1)} %constant_dynamic-update-slice_fusion.refs_1_.refs_2_), channel_id=1, source_target_pairs={{4,0},{5,1},{6,2},{7,3},{8,4},{9,5},{10,6},{11,7},{12,8},{13,9},{1... | collective-permute-start | bytes 2359304 | tf_op jit(solution)/shard_map/ppermute | solution.py:54
  29.8 14.3 %collective-permute-start.16 = (bf16[384,1024]{1,0:T(8,128)(2,1)S(1)}, bf16[384,1024]{1,0:T(8,128)(2,1)S(1)}, u32[]{:S(2)}, u32[]{:S(2)}) collective-permute-start(bf16[384,1024]{1,0:T(8,128)(2,1)S(1)} %constant_dynamic-update-slice_fusion.refs_1_.refs_2_), channel_id=1, source_target_pairs={{3,0},{0,1},{1,2},{2,3},{7,4},{4,5},{5,6},{6,7},{11,8},{8,9},{9,10... | collective-permute-start | bytes 2359304 | tf_op jit(solution)/shard_map/ppermute | solution.py:54
  31.1 16.0 %collective-permute-start.15 = (bf16[384,1024]{1,0:T(8,128)(2,1)S(1)}, bf16[384,1024]{1,0:T(8,128)(2,1)S(1)}, u32[]{:S(2)}, u32[]{:S(2)}) collective-permute-start(bf16[384,1024]{1,0:T(8,128)(2,1)S(1)} %collective-permute-done.14.refs_0_.refs_2_.refs_3_), channel_id=1, source_target_pairs={{4,0},{5,1},{6,2},{7,3},{8,4},{9,5},{10,6},{11,7},{12,8},{13,9},{1... | collective-permute-start | bytes 2359304 | tf_op jit(solution)/shard_map/ppermute | solution.py:54
  31.8 18.8 %collective-permute-start.12 = (bf16[384,1024]{1,0:T(8,128)(2,1)S(1)}, bf16[384,1024]{1,0:T(8,128)(2,1)S(1)}, u32[]{:S(2)}, u32[]{:S(2)}) collective-permute-start(bf16[384,1024]{1,0:T(8,128)(2,1)S(1)} %collective-permute-done.11.refs_4_), channel_id=1, source_target_pairs={{3,0},{0,1},{1,2},{2,3},{7,4},{4,5},{5,6},{6,7},{11,8},{8,9},{9,10... | collective-permute-start | bytes 2359304 | tf_op jit(solution)/shard_map/ppermute | solution.py:54
  38.3 13.7 %collective-permute-start.13 = (bf16[384,1024]{1,0:T(8,128)(2,1)S(1)}, bf16[384,1024]{1,0:T(8,128)(2,1)S(1)}, u32[]{:S(2)}, u32[]{:S(2)}) collective-permute-start(bf16[384,1024]{1,0:T(8,128)(2,1)S(1)} %collective-permute-done.10.refs_3_.refs_1_.refs_4_), channel_id=1, source_target_pairs={{1,0},{2,1},{3,2},{0,3},{5,4},{6,5},{7,6},{4,7},{9,8},{10,9},{11,1... | collective-permute-start | bytes 2359304 | tf_op jit(solution)/shard_map/ppermute | solution.py:54
  40.2 14.6 %collective-permute-start.5 = (bf16[384,1024]{1,0:T(8,128)(2,1)S(1)}, bf16[384,1024]{1,0:T(8,128)(2,1)S(1)}, u32[]{:S(2)}, u32[]{:S(2)}) collective-permute-start(bf16[384,1024]{1,0:T(8,128)(2,1)S(1)} %collective-permute-done.4.refs_0_.refs_3_.refs_4_), channel_id=1, source_target_pairs={{4,0},{5,1},{6,2},{7,3},{8,4},{9,5},{10,6},{11,7},{12,8},{13,9},{1... | collective-permute-start | bytes 2359304 | tf_op jit(solution)/shard_map/ppermute | solution.py:54

commit v2 on v1

--- a/solution.py
+++ b/solution.py
@@ -231,12 +231,12 @@
             found.append(got_ref[pl.ds(row + owner * 64, 1), :])
         row_ref[section : section + 1, :] = functools.reduce(jnp.maximum, found)
     columns = row_ref[...].T
-    best = jnp.full((1, rows), NONE, jnp.float32)
+    place = lax.broadcasted_iota(jnp.int32, (BOUND, rows), 0)
+    best = jnp.full((BOUND, rows), NONE, jnp.float32)
     for section in range(SECTIONS):
-        place = lax.broadcasted_iota(jnp.int32, (BOUND, rows), 0) + section * BOUND
-        found = jnp.where(slot_ref[...] == place, columns[:BOUND, section : section + 1], NONE)
-        best = jnp.maximum(best, jnp.max(found, 0, keepdims=True))
-    out_ref[...] = best
+        here_now = slot_ref[...] - section * BOUND == place
+        best = jnp.where(here_now, columns[:BOUND, section : section + 1], best)
+    out_ref[...] = jnp.max(best, 0, keepdims=True)
 
 
 def unsort(got, slot):

time: 77.5 us -> 77.5 us (level)
  no operation moved by 1% of the time
where the time goes in v2:
time: 77.5 us; the launch traced here: 77.3 us
  starting transfers between devices  23.5 us (30%)
  Pallas kernels  18.8 us (24%)
  blocking collectives  18.1 us (23%)
  waiting for transfers between devices  14.6 us (19%)
  local copies, waits for them, and re-layouts  2.07 us (3%)
    ppermute x17, starting transfers between devices, take(): return lax.ppermute(block, AXES, route)  23.5 us
    all_to_all x1, blocking collectives, on_device(): got = lax.all_to_all(best, AXES, 0, 0, tiled=True)  18.1 us
    pallas_call x9, Pallas kernels, pair_max(): pl.pallas_call(functools.partial(pair_kernel, names, blocks, products), i...  15.5 us
    ppermute x17, waiting for transfers between devices, take(): return lax.ppermute(block, AXES, route)  14.6 us
    unnamed x9, local copies, waits for them, and re-layouts  1.95 us
    pallas_call x1, Pallas kernels, unsort(): pl.pallas_call(unsort_kernel, in_specs=[vmem] * 2, out_specs=vmem, out_sh...  1.86 us
  transfers between devices with their start and end apart: 17, of which 7 were waited for; matrix products, arithmetic and copies ran while one was open for 0% of the time, Pallas kernels for 17%

profile of v2, /device:TPU:1, one launch (start us, length us, event | category | flops | bytes accessed | tf_op | source)
XLA Modules:
  0.0 77.3 jit_solution(6537028675829356470)
XLA Ops:
  0.0 1.2 %copy-done.1 = bf16[512,1024]{1,0:T(8,128)(2,1)S(1)} copy-done((bf16[512,1024]{1,0:T(8,128)(2,1)S(1)}, bf16[512,1024]{1,0:T(8,128)(2,1)}, u32[]{:S(2)}) %copy-start.1) | copy-done | bytes 1048600
  1.2 0.7 copy-done.2
  1.9 1.4 %sort_rows.1 = (bf16[384,1024]{1,0:T(8,128)(2,1)S(1)}, bf16[384,1024]{1,0:T(8,128)(2,1)S(1)}, s32[1,512]{1,0:T(1,128)S(1)}) custom-call(bf16[512,1024]{1,0:T(8,128)(2,1)S(1)} %copy-done.1, s32[1,512]{1,0:T(1,128)S(1)} %bitcast.7), custom_call_target="tpu_custom_call" | custom-call | flops 805306368 | bytes 3145728 | tf_op jit(solution)/shard_map/sort_rows/pallas_call | solution.py:103
  3.3 0.1 fusion
  3.4 2.1 %collective-permute-start.6 = (bf16[96,1024]{1,0:T(8,128)(2,1)S(1)}, bf16[96,1024]{1,0:T(8,128)(2,1)S(1)}, u32[]{:S(2)}, u32[]{:S(2)}) collective-permute-start(bf16[96,1024]{1,0:T(8,128)(2,1)S(1)} %get-tuple-element.14), channel_id=1, source_target_pairs={{48,0},{49,1},{50,2},{51,3},{52,4},{53,5},{54,6},{55,7},{56,8},{57... | collective-permute-start | bytes 589832 | tf_op jit(solution)/shard_map/ppermute | solution.py:54
  5.5 2.5 %collective-permute-start.7 = (bf16[96,1024]{1,0:T(8,128)(2,1)S(1)}, bf16[96,1024]{1,0:T(8,128)(2,1)S(1)}, u32[]{:S(2)}, u32[]{:S(2)}) collective-permute-start(bf16[96,1024]{1,0:T(8,128)(2,1)S(1)} %get-tuple-element.13), channel_id=1, source_target_pairs={{32,0},{33,1},{34,2},{35,3},{36,4},{37,5},{38,6},{39,7},{40,8},{41... | collective-permute-start | bytes 589832 | tf_op jit(solution)/shard_map/ppermute | solution.py:54
  7.9 1.2 %collective-permute-start.8 = (bf16[96,1024]{1,0:T(8,128)(2,1)S(1)}, bf16[96,1024]{1,0:T(8,128)(2,1)S(1)}, u32[]{:S(2)}, u32[]{:S(2)}) collective-permute-start(bf16[96,1024]{1,0:T(8,128)(2,1)S(1)} %get-tuple-element.12), channel_id=1, source_target_pairs={{16,0},{17,1},{18,2},{19,3},{20,4},{21,5},{22,6},{23,7},{24,8},{25... | collective-permute-start | bytes 589832 | tf_op jit(solution)/shard_map/ppermute | solution.py:54
  9.1 0.1 fusion.1
  9.2 2.5 %collective-permute-start = (bf16[96,1024]{1,0:T(8,128)(2,1)S(1)}, bf16[96,1024]{1,0:T(8,128)(2,1)S(1)}, u32[]{:S(2)}, u32[]{:S(2)}) collective-permute-start(bf16[96,1024]{1,0:T(8,128)(2,1)S(1)} %get-tuple-element.18), channel_id=1, source_target_pairs={{64,0},{65,1},{66,2},{67,3},{68,4},{69,5},{70,6},{71,7},{72,8},{73... | collective-permute-start | bytes 589832 | tf_op jit(solution)/shard_map/ppermute | solution.py:54
  11.6 0.7 collective-permute-start.1
  12.3 0.0 collective-permute-done.6
  12.3 1.8 %collective-permute-start.2 = (bf16[96,1024]{1,0:T(8,128)(2,1)S(1)}, bf16[96,1024]{1,0:T(8,128)(2,1)S(1)}, u32[]{:S(2)}, u32[]{:S(2)}) collective-permute-start(bf16[96,1024]{1,0:T(8,128)(2,1)S(1)} %get-tuple-element.16), channel_id=1, source_target_pairs={{96,0},{97,1},{98,2},{99,3},{100,4},{101,5},{102,6},{103,7},{104,8... | collective-permute-start | bytes 589832 | tf_op jit(solution)/shard_map/ppermute | solution.py:54
  14.1 0.0 collective-permute-done.7
  14.1 3.2 %collective-permute-start.3 = (bf16[96,1024]{1,0:T(8,128)(2,1)S(1)}, bf16[96,1024]{1,0:T(8,128)(2,1)S(1)}, u32[]{:S(2)}, u32[]{:S(2)}) collective-permute-start(bf16[96,1024]{1,0:T(8,128)(2,1)S(1)} %get-tuple-element.15), channel_id=1, source_target_pairs={{80,0},{81,1},{82,2},{83,3},{84,4},{85,5},{86,6},{87,7},{88,8},{89... | collective-permute-start | bytes 589832 | tf_op jit(solution)/shard_map/ppermute | solution.py:54
  17.3 0.0 collective-permute-done.8
  17.3 0.1 pad_maximum_fusion.refs_0_.refs_1_
  17.3 1.4 %collective-permute-start.14 = (bf16[384,1024]{1,0:T(8,128)(2,1)S(1)}, bf16[384,1024]{1,0:T(8,128)(2,1)S(1)}, u32[]{:S(2)}, u32[]{:S(2)}) collective-permute-start(bf16[384,1024]{1,0:T(8,128)(2,1)S(1)} %pad_maximum_fusion.refs_0_.refs_1_), channel_id=1, source_target_pairs={{4,0},{5,1},{6,2},{7,3},{8,4},{9,5},{10,6},{11,7},{12,8},{13,9},{1... | collective-permute-start | bytes 2359304 | tf_op jit(solution)/shard_map/ppermute | solution.py:54
  18.7 0.0 collective-permute-done
  18.7 0.6 collective-permute-start.9
  19.3 0.0 collective-permute-done.1
  19.3 0.9 %collective-permute-start.11 = (bf16[384,1024]{1,0:T(8,128)(2,1)S(1)}, bf16[384,1024]{1,0:T(8,128)(2,1)S(1)}, u32[]{:S(2)}, u32[]{:S(2)}) collective-permute-start(bf16[384,1024]{1,0:T(8,128)(2,1)S(1)} %pad_maximum_fusion.refs_0_.refs_1_), channel_id=1, source_target_pairs={{3,0},{0,1},{1,2},{2,3},{7,4},{4,5},{5,6},{6,7},{11,8},{8,9},{9,10... | collective-permute-start | bytes 2359304 | tf_op jit(solution)/shard_map/ppermute | solution.py:54
  20.3 0.7 collective-permute-done.2
  21.0 0.7 collective-permute-done.3
  21.8 1.6 %collective-permute-start.10 = (bf16[384,1024]{1,0:T(8,128)(2,1)S(1)}, bf16[384,1024]{1,0:T(8,128)(2,1)S(1)}, u32[]{:S(2)}, u32[]{:S(2)}) collective-permute-start(bf16[384,1024]{1,0:T(8,128)(2,1)S(1)} %constant_dynamic-update-slice_fusion.refs_1_.refs_2_), channel_id=1, source_target_pairs={{1,0},{2,1},{3,2},{0,3},{5,4},{6,5},{7,6},{4,7},{9,8},{10,9},{11,1... | collective-permute-start | bytes 2359304 | tf_op jit(solution)/shard_map/ppermute | solution.py:54
  23.4 1.3 %collective-permute-start.4 = (bf16[384,1024]{1,0:T(8,128)(2,1)S(1)}, bf16[384,1024]{1,0:T(8,128)(2,1)S(1)}, u32[]{:S(2)}, u32[]{:S(2)}) collective-permute-start(bf16[384,1024]{1,0:T(8,128)(2,1)S(1)} %constant_dynamic-update-slice_fusion.refs_1_.refs_2_), channel_id=1, source_target_pairs={{4,0},{5,1},{6,2},{7,3},{8,4},{9,5},{10,6},{11,7},{12,8},{13,9},{1... | collective-permute-start | bytes 2359304 | tf_op jit(solution)/shard_map/ppermute | solution.py:54
  24.7 1.5 %pair_max.9.refs_3_ = f32[6,768]{1,0:T(8,128)S(1)} custom-call(bf16[384,1024]{1,0:T(8,128)(2,1)S(1)} %pad_maximum_fusion.refs_0_.refs_1_, bf16[384,1024]{1,0:T(8,128)(2,1)S(1)} %constant_dynamic-update-slice_fusion.refs_1_.refs_2_, f32[6,768]{1,0:T(8,128)S(1)} %broadcast_in_dim.3.refs_2_), custom_call_target="tpu_custom_call" | custom-call | flops 7247757312 | bytes 1572864 | tf_op jit(solution)/shard_map/pair_max/pallas_call | solution.py:201
  26.2 3.6 %collective-permute-done.14.refs_0_.refs_2_.refs_3_ = bf16[384,1024]{1,0:T(8,128)(2,1)S(1)} collective-permute-done((bf16[384,1024]{1,0:T(8,128)(2,1)S(1)}, bf16[384,1024]{1,0:T(8,128)(2,1)S(1)}, u32[]{:S(2)}, u32[]{:S(2)}) %collective-permute-start.14) | collective-permute-done | bytes 786464 | tf_op jit(solution)/shard_map/ppermute | solution.py:54
  29.8 0.3 collective-permute-start.16
  30.1 1.0 %pair_max.10.refs_3_ = f32[6,768]{1,0:T(8,128)S(1)} custom-call(bf16[384,1024]{1,0:T(8,128)(2,1)S(1)} %collective-permute-done.14.refs_0_.refs_2_.refs_3_, bf16[384,1024]{1,0:T(8,128)(2,1)S(1)} %pad_maximum_fusion.refs_0_.refs_1_, bf16[384,1024]{1,0:T(8,128)(2,1)S(1)} %constant_dynamic-update-slice_fusion.refs_1_.refs_2_, f32[6,768]{1,0:T(8,128)S(1)} %pair_max.9.refs_3_), custom_call_target="tpu_custom_call" | custom-call | flops 3623878656 | bytes 2359296 | tf_op jit(solution)/shard_map/pair_max/pallas_call | solution.py:201
  31.1 0.1 collective-permute-start.15
  31.2 0.5 collective-permute-done.11.refs_4_
  31.8 0.2 collective-permute-start.12
  32.0 6.3 %collective-permute-done.10.refs_3_.refs_1_.refs_4_ = bf16[384,1024]{1,0:T(8,128)(2,1)S(1)} collective-permute-done((bf16[384,1024]{1,0:T(8,128)(2,1)S(1)}, bf16[384,1024]{1,0:T(8,128)(2,1)S(1)}, u32[]{:S(2)}, u32[]{:S(2)}) %collective-permute-start.10) | collective-permute-done | bytes 786464 | tf_op jit(solution)/shard_map/ppermute | solution.py:54
  38.3 1.9 %collective-permute-start.13 = (bf16[384,1024]{1,0:T(8,128)(2,1)S(1)}, bf16[384,1024]{1,0:T(8,128)(2,1)S(1)}, u32[]{:S(2)}, u32[]{:S(2)}) collective-permute-start(bf16[384,1024]{1,0:T(8,128)(2,1)S(1)} %collective-permute-done.10.refs_3_.refs_1_.refs_4_), channel_id=1, source_target_pairs={{1,0},{2,1},{3,2},{0,3},{5,4},{6,5},{7,6},{4,7},{9,8},{10,9},{11,1... | collective-permute-start | bytes 2359304 | tf_op jit(solution)/shard_map/ppermute | solution.py:54
  40.2 0.0 collective-permute-done.4.refs_0_.refs_3_.refs_4_
  40.2 1.3 %collective-permute-start.5 = (bf16[384,1024]{1,0:T(8,128)(2,1)S(1)}, bf16[384,1024]{1,0:T(8,128)(2,1)S(1)}, u32[]{:S(2)}, u32[]{:S(2)}) collective-permute-start(bf16[384,1024]{1,0:T(8,128)(2,1)S(1)} %collective-permute-done.4.refs_0_.refs_3_.refs_4_), channel_id=1, source_target_pairs={{4,0},{5,1},{6,2},{7,3},{8,4},{9,5},{10,6},{11,7},{12,8},{13,9},{1... | collective-permute-start | bytes 2359304 | tf_op jit(solution)/shard_map/ppermute | solution.py:54
  41.5 1.0 %pair_max.11.refs_4_ = f32[6,768]{1,0:T(8,128)S(1)} custom-call(bf16[384,1024]{1,0:T(8,128)(2,1)S(1)} %collective-permute-done.9.refs_0_.refs_3_, bf16[384,1024]{1,0:T(8,128)(2,1)S(1)} %pad_maximum_fusion.refs_0_.refs_1_, bf16[384,1024]{1,0:T(8,128)(2,1)S(1)} %constant_dynamic-update-slice_fusion.refs_1_.refs_2_, f32[6,768]{1,0:T(8,128)S(1)} %pair_max.10.refs_3_, ...), custom_call_target="tpu_custom_call" | custom-call | flops 3623878656 | bytes 2359296 | tf_op jit(solution)/shard_map/pair_max/pallas_call | solution.py:201
  42.4 1.6 %pair_max.12.refs_6_ = f32[6,768]{1,0:T(8,128)S(1)} custom-call(bf16[384,1024]{1,0:T(8,128)(2,1)S(1)} %collective-permute-done.4.refs_0_.refs_3_.refs_4_, bf16[384,1024]{1,0:T(8,128)(2,1)S(1)} %pad_maximum_fusion.refs_0_.refs_1_, bf16[384,1024]{1,0:T(8,128)(2,1)S(1)} %constant_dynamic-update-slice_fusion.refs_1_.refs_2_, ...), custom_call_target="tpu_custom_call" | custom-call | flops 7247757312 | bytes 3145728 | tf_op jit(solution)/shard_map/pair_max/pallas_call | solution.py:201
  44.1 0.0 collective-permute-done.16.refs_5_
  44.1 3.1 %pair_max.13.refs_5_ = f32[6,768]{1,0:T(8,128)S(1)} custom-call(bf16[384,1024]{1,0:T(8,128)(2,1)S(1)} %collective-permute-done.9.refs_0_.refs_3_, bf16[384,1024]{1,0:T(8,128)(2,1)S(1)} %collective-permute-done.10.refs_3_.refs_1_.refs_4_, bf16[384,1024]{1,0:T(8,128)(2,1)S(1)} %collective-permute-done.14.refs_0_.refs_2_.refs_3_, ...), custom_call_target="tpu_custom_call" | custom-call | flops 14495514624 | bytes 4718592 | tf_op jit(solution)/shard_map/pair_max/pallas_call | solution.py:201
  47.2 1.5 %pair_max.14.refs_5_ = f32[6,768]{1,0:T(8,128)S(1)} custom-call(bf16[384,1024]{1,0:T(8,128)(2,1)S(1)} %collective-permute-done.15.refs_0_.refs_5_, bf16[384,1024]{1,0:T(8,128)(2,1)S(1)} %pad_maximum_fusion.refs_0_.refs_1_, bf16[384,1024]{1,0:T(8,128)(2,1)S(1)} %constant_dynamic-update-slice_fusion.refs_1_.refs_2_, ...), custom_call_target="tpu_custom_call" | custom-call | flops 6039797760 | bytes 3932160 | tf_op jit(solution)/shard_map/pair_max/pallas_call | solution.py:201
  48.6 2.0 %collective-permute-done.12.refs_0_.refs_6_.refs_5_ = bf16[384,1024]{1,0:T(8,128)(2,1)S(1)} collective-permute-done((bf16[384,1024]{1,0:T(8,128)(2,1)S(1)}, bf16[384,1024]{1,0:T(8,128)(2,1)S(1)}, u32[]{:S(2)}, u32[]{:S(2)}) %collective-permute-start.12) | collective-permute-done | bytes 786464 | tf_op jit(solution)/shard_map/ppermute | solution.py:54
  50.6 1.4 %pair_max.15.refs_7_ = f32[6,768]{1,0:T(8,128)S(1)} custom-call(bf16[384,1024]{1,0:T(8,128)(2,1)S(1)} %collective-permute-done.12.refs_0_.refs_6_.refs_5_, bf16[384,1024]{1,0:T(8,128)(2,1)S(1)} %pad_maximum_fusion.refs_0_.refs_1_, bf16[384,1024]{1,0:T(8,128)(2,1)S(1)} %constant_dynamic-update-slice_fusion.refs_1_.refs_2_, ...), custom_call_target="tpu_custom_call" | custom-call | flops 6039797760 | bytes 3932160 | tf_op jit(solution)/shard_map/pair_max/pallas_call | solution.py:201
  52.0 2.1 %pair_max.16.refs_7_ = f32[6,768]{1,0:T(8,128)S(1)} custom-call(bf16[384,1024]{1,0:T(8,128)(2,1)S(1)} %collective-permute-done.13.refs_0_.refs_6_, bf16[384,1024]{1,0:T(8,128)(2,1)S(1)} %pad_maximum_fusion.refs_0_.refs_1_, bf16[384,1024]{1,0:T(8,128)(2,1)S(1)} %constant_dynamic-update-slice_fusion.refs_1_.refs_2_, ...), custom_call_target="tpu_custom_call" | custom-call | flops 9663676416 | bytes 5505024 | tf_op jit(solution)/shard_map/pair_max/pallas_call | solution.py:201
  54.1 0.7 collective-permute-done.5.refs_0_
  54.8 2.5 %pair_max.17 = f32[128,128]{1,0:T(8,128)S(1)} custom-call(bf16[384,1024]{1,0:T(8,128)(2,1)S(1)} %collective-permute-done.5.refs_0_, bf16[384,1024]{1,0:T(8,128)(2,1)S(1)} %pad_maximum_fusion.refs_0_.refs_1_, bf16[384,1024]{1,0:T(8,128)(2,1)S(1)} %constant_dynamic-update-slice_fusion.refs_1_.refs_2_, ...), custom_call_target="tpu_custom_call" | custom-call | flops 10871635968 | bytes 5505024 | tf_op jit(solution)/shard_map/pair_max/pallas_call | solution.py:201
  57.3 18.1 %all_to_all.11 = f32[128,1,128]{2,1,0:T(1,128)} all-to-all(f32[128,1,128]{2,1,0:T(1,128)S(1)} %bitcast.6), channel_id=1, replica_groups=mesh['group'=2,'member'=64] {'group','member'}, dimensions={0} | all-to-all | bytes 131072 | tf_op jit(solution)/shard_map/all_to_all | solution.py:296
  75.4 1.9 %unsort.1 = f32[1,512]{1,0:T(1,128)} custom-call(f32[128,128]{1,0:T(8,128)} %bitcast.8, s32[1,512]{1,0:T(1,128)} %copy-done), custom_call_target="tpu_custom_call" | custom-call | tf_op jit(solution)/shard_map/unsort/pallas_call | solution.py:244
  (12 shorter events, 0.1 us)
Async XLA Ops:
  0.0 1.2 %copy-start.1 = (bf16[512,1024]{1,0:T(8,128)(2,1)S(1)}, bf16[512,1024]{1,0:T(8,128)(2,1)}, u32[]{:S(2)}) copy-start(bf16[512,1024]{1,0:T(8,128)(2,1)} %rows_ref.1) | copy-start | bytes 3145732
  1.2 0.7 copy-start.2
  3.3 5.8 %copy-start = (s32[1,512]{1,0:T(1,128)}, s32[1,512]{1,0:T(1,128)S(1)}, u32[]{:S(2)}) copy-start(s32[1,512]{1,0:T(1,128)S(1)} %get-tuple-element.10.slot_ref) | copy-start | bytes 6148
  3.4 8.9 %collective-permute-start.6 = (bf16[96,1024]{1,0:T(8,128)(2,1)S(1)}, bf16[96,1024]{1,0:T(8,128)(2,1)S(1)}, u32[]{:S(2)}, u32[]{:S(2)}) collective-permute-start(bf16[96,1024]{1,0:T(8,128)(2,1)S(1)} %get-tuple-element.14), channel_id=1, source_target_pairs={{48,0},{49,1},{50,2},{51,3},{52,4},{53,5},{54,6},{55,7},{56,8},{57... | collective-permute-start | bytes 589832 | tf_op jit(solution)/shard_map/ppermute | solution.py:54
  5.5 8.6 %collective-permute-start.7 = (bf16[96,1024]{1,0:T(8,128)(2,1)S(1)}, bf16[96,1024]{1,0:T(8,128)(2,1)S(1)}, u32[]{:S(2)}, u32[]{:S(2)}) collective-permute-start(bf16[96,1024]{1,0:T(8,128)(2,1)S(1)} %get-tuple-element.13), channel_id=1, source_target_pairs={{32,0},{33,1},{34,2},{35,3},{36,4},{37,5},{38,6},{39,7},{40,8},{41... | collective-permute-start | bytes 589832 | tf_op jit(solution)/shard_map/ppermute | solution.py:54
  7.9 9.3 %collective-permute-start.8 = (bf16[96,1024]{1,0:T(8,128)(2,1)S(1)}, bf16[96,1024]{1,0:T(8,128)(2,1)S(1)}, u32[]{:S(2)}, u32[]{:S(2)}) collective-permute-start(bf16[96,1024]{1,0:T(8,128)(2,1)S(1)} %get-tuple-element.12), channel_id=1, source_target_pairs={{16,0},{17,1},{18,2},{19,3},{20,4},{21,5},{22,6},{23,7},{24,8},{25... | collective-permute-start | bytes 589832 | tf_op jit(solution)/shard_map/ppermute | solution.py:54
  9.2 9.6 %collective-permute-start = (bf16[96,1024]{1,0:T(8,128)(2,1)S(1)}, bf16[96,1024]{1,0:T(8,128)(2,1)S(1)}, u32[]{:S(2)}, u32[]{:S(2)}) collective-permute-start(bf16[96,1024]{1,0:T(8,128)(2,1)S(1)} %get-tuple-element.18), channel_id=1, source_target_pairs={{64,0},{65,1},{66,2},{67,3},{68,4},{69,5},{70,6},{71,7},{72,8},{73... | collective-permute-start | bytes 589832 | tf_op jit(solution)/shard_map/ppermute | solution.py:54
  11.6 7.7 %collective-permute-start.1 = (bf16[96,1024]{1,0:T(8,128)(2,1)S(1)}, bf16[96,1024]{1,0:T(8,128)(2,1)S(1)}, u32[]{:S(2)}, u32[]{:S(2)}) collective-permute-start(bf16[96,1024]{1,0:T(8,128)(2,1)S(1)} %get-tuple-element.17), channel_id=1, source_target_pairs={{112,0},{113,1},{114,2},{115,3},{116,4},{117,5},{118,6},{119,7},{1... | collective-permute-start | bytes 589832 | tf_op jit(solution)/shard_map/ppermute | solution.py:54
  12.3 8.7 %collective-permute-start.2 = (bf16[96,1024]{1,0:T(8,128)(2,1)S(1)}, bf16[96,1024]{1,0:T(8,128)(2,1)S(1)}, u32[]{:S(2)}, u32[]{:S(2)}) collective-permute-start(bf16[96,1024]{1,0:T(8,128)(2,1)S(1)} %get-tuple-element.16), channel_id=1, source_target_pairs={{96,0},{97,1},{98,2},{99,3},{100,4},{101,5},{102,6},{103,7},{104,8... | collective-permute-start | bytes 589832 | tf_op jit(solution)/shard_map/ppermute | solution.py:54
  14.1 7.7 %collective-permute-start.3 = (bf16[96,1024]{1,0:T(8,128)(2,1)S(1)}, bf16[96,1024]{1,0:T(8,128)(2,1)S(1)}, u32[]{:S(2)}, u32[]{:S(2)}) collective-permute-start(bf16[96,1024]{1,0:T(8,128)(2,1)S(1)} %get-tuple-element.15), channel_id=1, source_target_pairs={{80,0},{81,1},{82,2},{83,3},{84,4},{85,5},{86,6},{87,7},{88,8},{89... | collective-permute-start | bytes 589832 | tf_op jit(solution)/shard_map/ppermute | solution.py:54
  17.3 12.5 %collective-permute-start.14 = (bf16[384,1024]{1,0:T(8,128)(2,1)S(1)}, bf16[384,1024]{1,0:T(8,128)(2,1)S(1)}, u32[]{:S(2)}, u32[]{:S(2)}) collective-permute-start(bf16[384,1024]{1,0:T(8,128)(2,1)S(1)} %pad_maximum_fusion.refs_0_.refs_1_), channel_id=1, source_target_pairs={{4,0},{5,1},{6,2},{7,3},{8,4},{9,5},{10,6},{11,7},{12,8},{13,9},{1... | collective-permute-start | bytes 2359304 | tf_op jit(solution)/shard_map/ppermute | solution.py:54
  18.7 12.4 %collective-permute-start.9 = (bf16[384,1024]{1,0:T(8,128)(2,1)S(1)}, bf16[384,1024]{1,0:T(8,128)(2,1)S(1)}, u32[]{:S(2)}, u32[]{:S(2)}) collective-permute-start(bf16[384,1024]{1,0:T(8,128)(2,1)S(1)} %pad_maximum_fusion.refs_0_.refs_1_), channel_id=1, source_target_pairs={{1,0},{2,1},{3,2},{0,3},{5,4},{6,5},{7,6},{4,7},{9,8},{10,9},{11,1... | collective-permute-start | bytes 2359304 | tf_op jit(solution)/shard_map/ppermute | solution.py:54
  19.3 12.4 %collective-permute-start.11 = (bf16[384,1024]{1,0:T(8,128)(2,1)S(1)}, bf16[384,1024]{1,0:T(8,128)(2,1)S(1)}, u32[]{:S(2)}, u32[]{:S(2)}) collective-permute-start(bf16[384,1024]{1,0:T(8,128)(2,1)S(1)} %pad_maximum_fusion.refs_0_.refs_1_), channel_id=1, source_target_pairs={{3,0},{0,1},{1,2},{2,3},{7,4},{4,5},{5,6},{6,7},{11,8},{8,9},{9,10... | collective-permute-start | bytes 2359304 | tf_op jit(solution)/shard_map/ppermute | solution.py:54
  21.8 16.5 %collective-permute-start.10 = (bf16[384,1024]{1,0:T(8,128)(2,1)S(1)}, bf16[384,1024]{1,0:T(8,128)(2,1)S(1)}, u32[]{:S(2)}, u32[]{:S(2)}) collective-permute-start(bf16[384,1024]{1,0:T(8,128)(2,1)S(1)} %constant_dynamic-update-slice_fusion.refs_1_.refs_2_), channel_id=1, source_target_pairs={{1,0},{2,1},{3,2},{0,3},{5,4},{6,5},{7,6},{4,7},{9,8},{10,9},{11,1... | collective-permute-start | bytes 2359304 | tf_op jit(solution)/shard_map/ppermute | solution.py:54
  23.4 16.7 %collective-permute-start.4 = (bf16[384,1024]{1,0:T(8,128)(2,1)S(1)}, bf16[384,1024]{1,0:T(8,128)(2,1)S(1)}, u32[]{:S(2)}, u32[]{:S(2)}) collective-permute-start(bf16[384,1024]{1,0:T(8,128)(2,1)S(1)} %constant_dynamic-update-slice_fusion.refs_1_.refs_2_), channel_id=1, source_target_pairs={{4,0},{5,1},{6,2},{7,3},{8,4},{9,5},{10,6},{11,7},{12,8},{13,9},{1... | collective-permute-start | bytes 2359304 | tf_op jit(solution)/shard_map/ppermute | solution.py:54
  29.8 14.3 %collective-permute-start.16 = (bf16[384,1024]{1,0:T(8,128)(2,1)S(1)}, bf16[384,1024]{1,0:T(8,128)(2,1)S(1)}, u32[]{:S(2)}, u32[]{:S(2)}) collective-permute-start(bf16[384,1024]{1,0:T(8,128)(2,1)S(1)} %constant_dynamic-update-slice_fusion.refs_1_.refs_2_), channel_id=1, source_target_pairs={{3,0},{0,1},{1,2},{2,3},{7,4},{4,5},{5,6},{6,7},{11,8},{8,9},{9,10... | collective-permute-start | bytes 2359304 | tf_op jit(solution)/shard_map/ppermute | solution.py:54
  31.1 16.0 %collective-permute-start.15 = (bf16[384,1024]{1,0:T(8,128)(2,1)S(1)}, bf16[384,1024]{1,0:T(8,128)(2,1)S(1)}, u32[]{:S(2)}, u32[]{:S(2)}) collective-permute-start(bf16[384,1024]{1,0:T(8,128)(2,1)S(1)} %collective-permute-done.14.refs_0_.refs_2_.refs_3_), channel_id=1, source_target_pairs={{4,0},{5,1},{6,2},{7,3},{8,4},{9,5},{10,6},{11,7},{12,8},{13,9},{1... | collective-permute-start | bytes 2359304 | tf_op jit(solution)/shard_map/ppermute | solution.py:54
  31.8 18.8 %collective-permute-start.12 = (bf16[384,1024]{1,0:T(8,128)(2,1)S(1)}, bf16[384,1024]{1,0:T(8,128)(2,1)S(1)}, u32[]{:S(2)}, u32[]{:S(2)}) collective-permute-start(bf16[384,1024]{1,0:T(8,128)(2,1)S(1)} %collective-permute-done.11.refs_4_), channel_id=1, source_target_pairs={{3,0},{0,1},{1,2},{2,3},{7,4},{4,5},{5,6},{6,7},{11,8},{8,9},{9,10... | collective-permute-start | bytes 2359304 | tf_op jit(solution)/shard_map/ppermute | solution.py:54
  38.3 13.7 %collective-permute-start.13 = (bf16[384,1024]{1,0:T(8,128)(2,1)S(1)}, bf16[384,1024]{1,0:T(8,128)(2,1)S(1)}, u32[]{:S(2)}, u32[]{:S(2)}) collective-permute-start(bf16[384,1024]{1,0:T(8,128)(2,1)S(1)} %collective-permute-done.10.refs_3_.refs_1_.refs_4_), channel_id=1, source_target_pairs={{1,0},{2,1},{3,2},{0,3},{5,4},{6,5},{7,6},{4,7},{9,8},{10,9},{11,1... | collective-permute-start | bytes 2359304 | tf_op jit(solution)/shard_map/ppermute | solution.py:54
  40.2 14.6 %collective-permute-start.5 = (bf16[384,1024]{1,0:T(8,128)(2,1)S(1)}, bf16[384,1024]{1,0:T(8,128)(2,1)S(1)}, u32[]{:S(2)}, u32[]{:S(2)}) collective-permute-start(bf16[384,1024]{1,0:T(8,128)(2,1)S(1)} %collective-permute-done.4.refs_0_.refs_3_.refs_4_), channel_id=1, source_target_pairs={{4,0},{5,1},{6,2},{7,3},{8,4},{9,5},{10,6},{11,7},{12,8},{13,9},{1... | collective-permute-start | bytes 2359304 | tf_op jit(solution)/shard_map/ppermute | solution.py:54
